TPU v7x, 256 devices: a whole 4x4x8 slice. The times are simulated.
256 devices in a mesh: ctx: 32 (over y, x, core), head: 8 (over z).
Axes of the slice: x: 4, y: 4, z: 8, core: 2. Of those that a mesh axis runs over, the one named last changes fastest.
Arguments:
- queries: bfloat16 [4096, 24576], P('ctx', 'head'), may hold values from -120 to 120
- latents: bfloat16 [4096, 576], P('ctx'), may hold values from -6 to 6
- w_uk: bfloat16 [512, 16384], P(None, 'head'), may hold values from -0.5 to 0.5
- w_uv: bfloat16 [512, 16384], P(None, 'head'), may hold values from -0.25 to 0.25
- out_grad: bfloat16 [4096, 16384], P('ctx', 'head'), may hold values from -6 to 6
- doc_ids: int32 [4096], P('ctx'), may hold values from 0 to 8192, as said below
Outputs:
- attn_output: bfloat16 [4096, 16384], P('ctx', 'head')
- query_grad: float32 [4096, 24576], P('ctx', 'head')
- latent_grad: float32 [4096, 576], P('ctx')
- w_uk_grad: float32 [512, 16384], P('ctx', 'head')
- w_uv_grad: float32 [512, 16384], P('ctx', 'head')
Inputs may be any that keep to these rules, and one draw needn't show every extreme that they name: `doc_ids`: document numbers never fall along the window; every document is a run of 1 to 448 tokens, and one holds exactly 448.
All inputs are finite; a program needn't handle non-finite values.
Results may differ from a plain program's by a relative error of at most 0.012.
Values may be sent and summed in bfloat16 or wider, within the bound.
No kernel may reach another device: no remote copies, remote signals or barrier semaphores. Data moves between devices by JAX's collectives and lax.ppermute only.
A program may use at most 128 MiB of HBM per device.

v0:
```python
import jax
import jax.numpy as jnp
from jax import lax
from jax.sharding import PartitionSpec as P

LATENT = 512
ROPE = 64
NOPE = 128
SPAN = 4


masked_value = -1e30


def passed_along(x, axis, by):
    peers = lax.axis_size(axis)
    pairs = [(i, i + by) for i in range(peers) if 0 <= i + by < peers]
    return lax.ppermute(x, axis, pairs)


def attend(query_blk, grad_blk, key_rows, visible, w_uk, w_uv):
    head_count = query_blk.shape[1]
    q_nope = query_blk[:, :, :NOPE]
    q_rope = query_blk[:, :, NOPE:]
    c_nope = key_rows[:, :LATENT]
    k_rope = key_rows[:, LATENT:]
    up_key = w_uk.reshape(LATENT, head_count, NOPE)
    up_value = w_uv.reshape(LATENT, head_count, NOPE)
    softmax_scale = (NOPE + ROPE) ** (-0.5)
    f32 = jnp.float32
    absorbed = jnp.einsum("thd,lhd->thl", q_nope, up_key, preferred_element_type=f32).astype(
        jnp.bfloat16
    )
    scores = (
        jnp.einsum("thl,ul->thu", absorbed, c_nope, preferred_element_type=f32)
        + jnp.einsum("thr,ur->thu", q_rope, k_rope, preferred_element_type=f32)
    ) * softmax_scale
    allowed = visible[:, None, :]
    scores = jnp.where(allowed, scores, masked_value)
    top_score = jnp.max(scores, axis=-1, keepdims=True)
    exp_terms = jnp.where(allowed, jnp.exp(scores - top_score), 0.0)
    attn_probs = exp_terms / jnp.sum(exp_terms, axis=-1, keepdims=True)
    probs_bf = attn_probs.astype(jnp.bfloat16)
    attended = jnp.einsum("thu,ul->thl", probs_bf, c_nope, preferred_element_type=f32).astype(
        jnp.bfloat16
    )
    attn_out = jnp.einsum("thl,lhd->thd", attended, up_value, preferred_element_type=f32).astype(
        jnp.bfloat16
    )
    grad_latent = jnp.einsum("thd,lhd->thl", grad_blk, up_value, preferred_element_type=f32).astype(
        jnp.bfloat16
    )
    grad_probs = jnp.einsum("thl,ul->thu", grad_latent, c_nope, preferred_element_type=f32)
    row_delta = jnp.sum(attn_probs * grad_probs, axis=-1, keepdims=True)
    grad_scores = (attn_probs * (grad_probs - row_delta) * softmax_scale).astype(jnp.bfloat16)
    grad_absorbed = jnp.einsum(
        "thu,ul->thl", grad_scores, c_nope, preferred_element_type=f32
    ).astype(jnp.bfloat16)
    grad_qrope = jnp.einsum("thu,ur->thr", grad_scores, k_rope, preferred_element_type=f32)
    grad_qnope = jnp.einsum("thl,lhd->thd", grad_absorbed, up_key, preferred_element_type=f32)
    grad_query = jnp.concatenate([grad_qnope, grad_qrope], axis=-1)
    grad_cnope = jnp.einsum(
        "thu,thl->ul", probs_bf, grad_latent, preferred_element_type=f32
    ) + jnp.einsum("thu,thl->ul", grad_scores, absorbed, preferred_element_type=f32)
    grad_krope = jnp.einsum("thu,thr->ur", grad_scores, q_rope, preferred_element_type=f32)
    grad_keys = jnp.concatenate([grad_cnope, grad_krope], axis=-1)
    return (attn_out, grad_query, grad_keys, grad_absorbed, attended, q_nope)


def body(queries, latents, w_uk, w_uv, out_grad, doc_ids):
    tok_rows = latents.shape[0]
    head_count = w_uk.shape[1] // NOPE
    ctx_index = lax.axis_index("ctx")
    lat_blocks = [latents]
    id_blocks = [doc_ids]
    for distance in range(1, SPAN + 1):
        moved_lat, moved_ids = passed_along((latents, doc_ids), "ctx", distance)
        lat_blocks.append(moved_lat)
        id_blocks.append(moved_ids)
    key_rows = jnp.concatenate(lat_blocks, axis=0)
    key_ids = jnp.concatenate(id_blocks, axis=0)
    offsets = jnp.arange(tok_rows, dtype=jnp.int32)
    query_pos = ctx_index * tok_rows + offsets
    key_pos = jnp.concatenate(
        [(ctx_index - distance) * tok_rows + offsets for distance in range(SPAN + 1)], axis=0
    )
    visible = (
        (key_ids[None, :] == doc_ids[:, None])
        & (key_pos[None, :] <= query_pos[:, None])
        & (key_pos[None, :] >= 0)
    )
    query_blk = queries.reshape(tok_rows, head_count, NOPE + ROPE)
    grad_blk = out_grad.reshape(tok_rows, head_count, NOPE)
    attn_out, grad_query, grad_keys, grad_absorbed, attended, q_nope = attend(
        query_blk, grad_blk, key_rows, visible, w_uk, w_uv
    )
    pieces = [
        grad_keys[distance * tok_rows : (distance + 1) * tok_rows] for distance in range(SPAN + 1)
    ]
    grad_total = pieces[0]
    for distance in range(1, SPAN + 1):
        grad_total = grad_total + passed_along(
            pieces[distance].astype(jnp.bfloat16), "ctx", -distance
        ).astype(jnp.float32)
    grad_total = lax.psum(grad_total, "head")
    wgt_terms = jnp.concatenate(
        [
            jnp.einsum(
                "thl,thd->lhd", grad_absorbed, q_nope, preferred_element_type=jnp.float32
            ).reshape(LATENT, head_count * NOPE),
            jnp.einsum(
                "thl,thd->lhd", attended, grad_blk, preferred_element_type=jnp.float32
            ).reshape(LATENT, head_count * NOPE),
        ],
        axis=1,
    )
    own_rows = lax.psum_scatter(wgt_terms, "ctx", scatter_dimension=0, tiled=True)
    grad_wk = own_rows[:, : head_count * NOPE]
    grad_wv = own_rows[:, head_count * NOPE :]
    return (
        attn_out.reshape(tok_rows, head_count * NOPE),
        grad_query.reshape(tok_rows, head_count * (NOPE + ROPE)),
        grad_total,
        grad_wk,
        grad_wv,
    )


def solution(mesh):
    placed = (
        P("ctx", "head"),
        P("ctx", None),
        P(None, "head"),
        P(None, "head"),
        P("ctx", "head"),
        P("ctx"),
    )
    return jax.shard_map(
        body,
        mesh=mesh,
        in_specs=placed,
        out_specs=(
            P("ctx", "head"),
            P("ctx", "head"),
            P("ctx", None),
            P("ctx", "head"),
            P("ctx", "head"),
        ),
        check_vma=False,
    )
```

profile of v0, /device:TPU:32, one launch (start us, length us, event | category | flops | bytes accessed | tf_op | source)
XLA Modules:
  0.0 294.6 jit_solution(8023181449448531252)
XLA Ops:
  8.0 0.0 copy-start
  8.0 0.0 reduce-scatter.2.cloned.1.call-start
  8.1 5.1 %collective-permute-start.3 = (s32[128]{0:T(128)}, s32[128]{0:T(128)S(1)}, u32[]{:S(2)}, u32[]{:S(2)}) collective-permute-start(s32[128]{0:T(128)} %param.11), channel_id=1, source_target_pairs={{0,32},{8,40},{16,48},{24,56},{32,64},{40,72},{48,80},{56,88},{64,... | collective-permute-start | bytes 1544 | tf_op jit(solution)/shard_map/ppermute | solution.py:18
  13.1 1.7 collective-permute-start.2
  14.8 2.8 collective-permute-start.1
  17.6 4.1 %collective-permute-start = (s32[128]{0:T(128)}, s32[128]{0:T(128)S(1)}, u32[]{:S(2)}, u32[]{:S(2)}) collective-permute-start(s32[128]{0:T(128)} %param.11), channel_id=1, source_target_pairs={{0,8},{8,16},{16,24},{24,32},{32,40},{40,48},{48,56},{56,64},{64,7... | collective-permute-start | bytes 1544 | tf_op jit(solution)/shard_map/ppermute | solution.py:18
  21.7 1.7 copy.41
  23.4 5.3 %collective-permute-start.7 = (bf16[128,576]{1,0:T(8,128)(2,1)}, bf16[128,576]{1,0:T(8,128)(2,1)}, u32[]{:S(2)}, u32[]{:S(2)}) collective-permute-start(bf16[128,576]{1,0:T(8,128)(2,1)} %copy.41), channel_id=1, source_target_pairs={{0,32},{8,40},{16,48},{24,56},{32,64},{40,72},{48,80},{56,88},{64,... | collective-permute-start | bytes 442376 | tf_op jit(solution)/shard_map/ppermute | solution.py:18
  28.7 1.6 constant_dynamic-update-slice_fusion.6
  30.4 1.3 copy.67
  31.7 1.5 copy.34
  33.2 3.9 %copy.66 = bf16[512,2048]{0,1:T(8,128)(2,1)} copy(bf16[512,2048]{1,0:T(8,128)(2,1)} %param.8) | data formatting | bytes 4194304 | tf_op jit(solution)/shard_map/reshape | solution.py:27
  37.2 0.7 fusion.32
  37.9 0.9 copy-done.1
  38.8 2.1 convolution_convert_fusion.1
  40.9 0.0 collective-permute-done
  40.9 2.1 collective-permute-start.6
  43.1 0.0 collective-permute-done.1
  43.1 2.2 collective-permute-start.5
  45.3 0.0 collective-permute-done.2
  45.3 3.9 %collective-permute-start.4 = (bf16[128,576]{1,0:T(8,128)(2,1)}, bf16[128,576]{1,0:T(8,128)(2,1)S(1)}, u32[]{:S(2)}, u32[]{:S(2)}) collective-permute-start(bf16[128,576]{1,0:T(8,128)(2,1)} %copy.41), channel_id=1, source_target_pairs={{0,8},{8,16},{16,24},{24,32},{32,40},{40,48},{48,56},{56,64},{64,7... | collective-permute-start | bytes 442376 | tf_op jit(solution)/shard_map/ppermute | solution.py:18
  49.3 0.0 collective-permute-done.3
  49.3 0.1 and_and_fusion
  49.5 1.0 collective-permute-done.4
  50.5 0.6 collective-permute-done.5
  51.2 0.0 collective-permute-done.6
  51.2 0.9 constant_dynamic-update-slice_fusion.2
  52.2 3.2 %fusion.68 = f32[640,128,16]{0,1,2:T(8,128)} fusion(bf16[128,16,192]{0,2,1:T(8,128)(2,1)S(1)} %bitcast.92, bf16[640,576]{1,0:T(8,128)(2,1)S(1)} %constant_dynamic-update-slice_fusion.2), kind=kOutput, calls=%fused_computation.55 | convolution fusion | flops 167772160 | bytes 5668864 | tf_op jit(solution)/shard_map/thr,ur->thu/dot_general | solution.py:36
  55.4 4.1 %fusion.25 = f32[128,16,640]{2,0,1:T(8,128)} fusion(bf16[16,512,128]{2,1,0:T(8,128)(2,1)S(1)} %fusion.32, bf16[640,576]{1,0:T(8,128)(2,1)S(1)} %constant_dynamic-update-slice_fusion.2), kind=kOutput, calls=%fused_computation.21 | convolution fusion | flops 1342177280 | bytes 7995392 | tf_op jit(solution)/shard_map/thl,ul->thu/dot_general | solution.py:53
  59.5 9.3 %fusion.80 = (f32[128,16]{0,1:T(8,128)S(1)}, f32[128,16,640]{2,0,1:T(8,128)}) fusion(pred[128,640]{1,0:T(8,128)(4,1)S(1)} %and_and_fusion, f32[640,128,16]{0,1,2:T(8,128)} %fusion.68, bf16[16,512,128]{2,1,0:T(8,128)(2,1)} %convolution_convert_fusion.1, bf16[640,576]{1,0:T(8,128)(2,1)} %copy-done.6), kind=kOutput, calls=%fused_computation.85 | convolution fusion | flops 1350042240 | bytes 13410304 | tf_op jit(solution)/shard_map/sub | solution.py:41
  68.8 5.8 %convolution_convert_fusion = bf16[128,16,512]{2,0,1:T(8,128)(2,1)} fusion(bf16[640,576]{1,0:T(8,128)(2,1)} %copy-done.6, f32[128,16,640]{2,0,1:T(8,128)} %get-tuple-element.22, f32[128,16]{0,1:T(8,128)S(1)} %get-tuple-element.21), kind=kOutput, calls=%fused_computation.28 | convolution fusion | flops 1345847296 | bytes 8003584 | tf_op jit(solution)/shard_map/thu,ul->thl/dot_general | solution.py:44
  74.6 15.0 %fusion.29 = bf16[128,16,512]{2,0,1:T(8,128)(2,1)} fusion(f32[128,16,640]{2,0,1:T(8,128)} %fusion.25, bf16[640,576]{1,0:T(8,128)(2,1)} %copy-done.6, f32[128,16,640]{2,0,1:T(8,128)} %get-tuple-element.22, f32[128,16]{0,1:T(8,128)S(1)} %get-tuple-element.21), kind=kOutput, calls=%fused_computation.27 | convolution fusion | flops 1352403584 | bytes 23740416 | tf_op jit(solution)/shard_map/thu,ul->thl/dot_general | solution.py:56
  89.6 4.2 %fusion.60 = f32[16,512,128]{1,2,0:T(8,128)} fusion(bf16[128,16,512]{2,0,1:T(8,128)(2,1)} %fusion.29, bf16[128,16,192]{0,2,1:T(8,128)(2,1)S(1)} %bitcast.93), kind=kOutput, calls=%fused_computation.46 | convolution fusion | flops 268435456 | bytes 6815744 | tf_op jit(solution)/shard_map/thl,thd->lhd/dot_general | solution.py:108
  93.9 5.4 %copy.53 = f32[512,2048]{1,0:T(8,128)} copy(f32[512,2048]{0,1:T(8,128)} %bitcast.89) | data formatting | bytes 8388608 | tf_op jit(solution)/shard_map/reshape | solution.py:110
  99.3 4.2 %fusion.83 = f32[16,512,128]{1,2,0:T(8,128)} fusion(bf16[128,16,128]{0,2,1:T(8,128)(2,1)S(1)} %bitcast.96, bf16[128,16,512]{2,0,1:T(8,128)(2,1)} %convolution_convert_fusion), kind=kOutput, calls=%fused_computation.86 | convolution fusion | flops 268435456 | bytes 6815744 | tf_op jit(solution)/shard_map/thl,thd->lhd/dot_general | solution.py:111
  103.5 5.4 %copy.54 = f32[512,2048]{1,0:T(8,128)} copy(f32[512,2048]{0,1:T(8,128)} %bitcast.88) | data formatting | bytes 8388608 | tf_op jit(solution)/shard_map/reshape | solution.py:113
  108.9 7.7 %pad_maximum_fusion = f32[512,4096]{1,0:T(8,128)} fusion(f32[512,2048]{1,0:T(8,128)} %copy.54, f32[512,2048]{1,0:T(8,128)} %copy.53), kind=kLoop, calls=%fused_computation.2 | loop fusion | flops 2097152 | bytes 16777216 | tf_op jit(solution)/shard_map/concatenate | solution.py:106
  116.6 0.0 reduce-scatter.2.cloned.1.call-update
  116.6 0.0 all-reduce.2.cloned.1.call-start
  116.6 18.9 %fusion.56 = f32[640,64]{0,1:T(8,128)} fusion(f32[128,16,640]{2,0,1:T(8,128)} %fusion.25, bf16[128,16,192]{0,2,1:T(8,128)(2,1)S(1)} %bitcast.94, f32[128,16,640]{2,0,1:T(8,128)} %get-tuple-element.22, f32[128,16]{0,1:T(8,128)S(1)} %get-tuple-element.21), kind=kOutput, calls=%fused_computation.43 | convolution fusion | flops 176949888 | bytes 21413888 | tf_op jit(solution)/shard_map/thu,thr->ur/dot_general | solution.py:65
  135.5 6.4 %fusion.38 = f32[640,512]{0,1:T(8,128)} fusion(bf16[16,512,128]{2,1,0:T(8,128)(2,1)} %copy-done.4, f32[128,16,640]{2,0,1:T(8,128)} %get-tuple-element.22, f32[128,16]{0,1:T(8,128)S(1)} %get-tuple-element.21), kind=kOutput, calls=%fused_computation.36 | convolution fusion | flops 1344798720 | bytes 8658944 | tf_op jit(solution)/shard_map/thu,thl->ul/dot_general | solution.py:62
  142.0 19.7 %fusion.46 = f32[640,512]{0,1:T(8,128)S(1)} fusion(f32[640,512]{0,1:T(8,128)} %fusion.38, f32[128,16,640]{2,0,1:T(8,128)} %fusion.25, bf16[16,512,128]{2,1,0:T(8,128)(2,1)} %convolution_convert_fusion.1, f32[128,16,640]{2,0,1:T(8,128)} %get-tuple-element.22, f32[128,16]{0,1:T(8,128)S(1)} %get-tuple-element.21), kind=kOutput, calls=%fused_computation.39 | convolution fusion | flops 1351682688 | bytes 15212544 | tf_op jit(solution)/shard_map/thu,thl->ul/dot_general | solution.py:64
  161.7 1.0 fusion.37
  162.7 0.9 fusion.78
  163.5 1.3 collective-permute-start.8
  164.8 1.3 collective-permute-start.11
  166.1 1.3 collective-permute-start.10
  167.4 1.3 collective-permute-start.9
  168.7 18.9 %fusion.14 = f32[128,16,64]{0,2,1:T(8,128)} fusion(f32[128,16,640]{2,0,1:T(8,128)} %fusion.25, bf16[640,576]{1,0:T(8,128)(2,1)} %copy-done.6, f32[128,16,640]{2,0,1:T(8,128)} %get-tuple-element.22, f32[128,16]{0,1:T(8,128)} %copy-done.9), kind=kOutput, calls=%fused_computation.13 | convolution fusion | flops 176949888 | bytes 21676032 | tf_op jit(solution)/shard_map/thu,ur->thr/dot_general | solution.py:59
  187.7 0.0 copy-start.7
  187.7 3.3 %fusion.53 = bf16[16,128,128]{1,2,0:T(8,128)(2,1)} fusion(bf16[128,16,512]{2,0,1:T(8,128)(2,1)} %convolution_convert_fusion, bf16[512,2048]{1,0:T(8,128)(2,1)S(1)} %copy-done), kind=kOutput, calls=%fused_computation.42 | convolution fusion | flops 268697600 | bytes 4718592 | tf_op jit(solution)/shard_map/thl,lhd->thd/dot_general | solution.py:47
  191.0 0.7 convolution_bitcast_fusion
  191.7 1.3 pad_maximum_fusion.2
  193.0 3.0 %copy.56 = f32[128,3072]{1,0:T(8,128)} copy(f32[128,3072]{0,1:T(8,128)} %bitcast.90) | data formatting | bytes 3145728
  196.1 2.0 copy.55
  198.1 0.0 collective-permute-done.8
  198.1 0.0 collective-permute-done.11
  198.1 0.0 collective-permute-done.9
  198.1 1.9 fusion.66
  200.0 0.0 all-reduce.2.cloned.1.call-update
  200.0 29.1 %reduce-scatter.2.cloned.1.call-done = f32[16,4096]{1,0:T(8,128)} async-done(((f32[512,4096]{1,0:T(8,128)}), f32[16,4096]{1,0:T(8,128)}) %reduce-scatter.2.cloned.1.call-update) | async-done | bytes 262160 | tf_op jit(solution)/shard_map/reduce_scatter | solution.py:117
  229.2 1.7 fusion.79
  230.8 54.6 %all-reduce.2.cloned.1.call-done = f32[128,576]{0,1:T(8,128)} async-done(((f32[128,576]{0,1:T(8,128)}), f32[128,576]{0,1:T(8,128)}) %all-reduce.2.cloned.1.call-update) | async-done | bytes 294928 | tf_op jit(solution)/shard_map/psum | solution.py:105
  285.5 1.7 copy.94
  (35 shorter events, 0.2 us)
Async XLA Ops:
  8.0 29.2 %copy-start = (bf16[512,2048]{1,0:T(8,128)(2,1)S(1)}, bf16[512,2048]{1,0:T(8,128)(2,1)}, u32[]{:S(2)}) copy-start(bf16[512,2048]{1,0:T(8,128)(2,1)} %param.9) | copy-start | bytes 6291460
  8.0 221.1 %reduce-scatter.2.cloned.1.call-start = ((), (), s32[]{:S(2)}) async-start(), calls=%async_computation.2 | async-start | bytes 8650752 | tf_op jit(solution)/shard_map/reduce_scatter | solution.py:117
  8.1 41.2 %collective-permute-start.3 = (s32[128]{0:T(128)}, s32[128]{0:T(128)S(1)}, u32[]{:S(2)}, u32[]{:S(2)}) collective-permute-start(s32[128]{0:T(128)} %param.11), channel_id=1, source_target_pairs={{0,32},{8,40},{16,48},{24,56},{32,64},{40,72},{48,80},{56,88},{64,... | collective-permute-start | bytes 1544 | tf_op jit(solution)/shard_map/ppermute | solution.py:18
  13.1 32.2 %collective-permute-start.2 = (s32[128]{0:T(128)}, s32[128]{0:T(128)S(1)}, u32[]{:S(2)}, u32[]{:S(2)}) collective-permute-start(s32[128]{0:T(128)} %param.11), channel_id=1, source_target_pairs={{0,24},{8,32},{16,40},{24,48},{32,56},{40,64},{48,72},{56,80},{64,... | collective-permute-start | bytes 1544 | tf_op jit(solution)/shard_map/ppermute | solution.py:18
  14.8 28.3 %collective-permute-start.1 = (s32[128]{0:T(128)}, s32[128]{0:T(128)S(1)}, u32[]{:S(2)}, u32[]{:S(2)}) collective-permute-start(s32[128]{0:T(128)} %param.11), channel_id=1, source_target_pairs={{0,16},{8,24},{16,32},{24,40},{32,48},{40,56},{48,64},{56,72},{64,... | collective-permute-start | bytes 1544 | tf_op jit(solution)/shard_map/ppermute | solution.py:18
  17.6 23.3 %collective-permute-start = (s32[128]{0:T(128)}, s32[128]{0:T(128)S(1)}, u32[]{:S(2)}, u32[]{:S(2)}) collective-permute-start(s32[128]{0:T(128)} %param.11), channel_id=1, source_target_pairs={{0,8},{8,16},{16,24},{24,32},{32,40},{40,48},{48,56},{56,64},{64,7... | collective-permute-start | bytes 1544 | tf_op jit(solution)/shard_map/ppermute | solution.py:18
  23.4 27.8 %collective-permute-start.7 = (bf16[128,576]{1,0:T(8,128)(2,1)}, bf16[128,576]{1,0:T(8,128)(2,1)}, u32[]{:S(2)}, u32[]{:S(2)}) collective-permute-start(bf16[128,576]{1,0:T(8,128)(2,1)} %copy.41), channel_id=1, source_target_pairs={{0,32},{8,40},{16,48},{24,56},{32,64},{40,72},{48,80},{56,88},{64,... | collective-permute-start | bytes 442376 | tf_op jit(solution)/shard_map/ppermute | solution.py:18
  37.2 1.6 copy-start.1
  37.2 3.7 %copy-start.8 = (s32[128]{0:T(128)S(1)}, s32[128]{0:T(128)}, u32[]{:S(2)}) copy-start(s32[128]{0:T(128)} %param.11) | copy-start | bytes 1540
  37.2 13.3 %copy-start.5 = (bf16[640,576]{1,0:T(8,128)(2,1)S(1)}, bf16[640,576]{1,0:T(8,128)(2,1)}, u32[]{:S(2)}) copy-start(bf16[640,576]{1,0:T(8,128)(2,1)} %constant_dynamic-update-slice_fusion.6) | copy-start | bytes 2211844
  37.9 17.5 %copy-start.4 = (bf16[16,512,128]{2,1,0:T(8,128)(2,1)}, bf16[16,512,128]{2,1,0:T(8,128)(2,1)S(1)}, u32[]{:S(2)}) copy-start(bf16[16,512,128]{2,1,0:T(8,128)(2,1)S(1)} %fusion.32) | copy-start | bytes 6291460
  40.9 10.2 %collective-permute-start.6 = (bf16[128,576]{1,0:T(8,128)(2,1)}, bf16[128,576]{1,0:T(8,128)(2,1)S(1)}, u32[]{:S(2)}, u32[]{:S(2)}) collective-permute-start(bf16[128,576]{1,0:T(8,128)(2,1)} %copy.41), channel_id=1, source_target_pairs={{0,24},{8,32},{16,40},{24,48},{32,56},{40,64},{48,72},{56,80},{64,... | collective-permute-start | bytes 442376 | tf_op jit(solution)/shard_map/ppermute | solution.py:18
  43.1 8.1 %collective-permute-start.5 = (bf16[128,576]{1,0:T(8,128)(2,1)}, bf16[128,576]{1,0:T(8,128)(2,1)S(1)}, u32[]{:S(2)}, u32[]{:S(2)}) collective-permute-start(bf16[128,576]{1,0:T(8,128)(2,1)} %copy.41), channel_id=1, source_target_pairs={{0,16},{8,24},{16,32},{24,40},{32,48},{40,56},{48,64},{56,72},{64,... | collective-permute-start | bytes 442376 | tf_op jit(solution)/shard_map/ppermute | solution.py:18
  45.3 5.2 %collective-permute-start.4 = (bf16[128,576]{1,0:T(8,128)(2,1)}, bf16[128,576]{1,0:T(8,128)(2,1)S(1)}, u32[]{:S(2)}, u32[]{:S(2)}) collective-permute-start(bf16[128,576]{1,0:T(8,128)(2,1)} %copy.41), channel_id=1, source_target_pairs={{0,8},{8,16},{16,24},{24,32},{32,40},{40,48},{48,56},{56,64},{64,7... | collective-permute-start | bytes 442376 | tf_op jit(solution)/shard_map/ppermute | solution.py:18
  52.2 3.2 %copy-start.6 = (bf16[640,576]{1,0:T(8,128)(2,1)}, bf16[640,576]{1,0:T(8,128)(2,1)S(1)}, u32[]{:S(2)}) copy-start(bf16[640,576]{1,0:T(8,128)(2,1)S(1)} %constant_dynamic-update-slice_fusion.2) | copy-start | bytes 2211844
  68.8 73.2 %copy-start.9 = (f32[128,16]{0,1:T(8,128)}, f32[128,16]{0,1:T(8,128)S(1)}, u32[]{:S(2)}) copy-start(f32[128,16]{0,1:T(8,128)S(1)} %get-tuple-element.21) | copy-start | bytes 24580
  116.6 168.9 %all-reduce.2.cloned.1.call-start = ((), (), s32[]{:S(2)}) async-start(), calls=%async_computation.1 | async-start | bytes 589824 | tf_op jit(solution)/shard_map/psum | solution.py:105
  163.5 34.6 %collective-permute-start.8 = (bf16[128,576]{0,1:T(8,128)(2,1)}, bf16[128,576]{0,1:T(8,128)(2,1)S(1)}, u32[]{:S(2)}, u32[]{:S(2)}) collective-permute-start(bf16[128,576]{0,1:T(8,128)(2,1)} %get-tuple-element.15), channel_id=1, source_target_pairs={{8,0},{16,8},{24,16},{32,24},{40,32},{48,40},{56,48},{64,56},{72,6... | collective-permute-start | bytes 442376 | tf_op jit(solution)/shard_map/ppermute | solution.py:18
  164.8 33.3 %collective-permute-start.11 = (bf16[128,576]{0,1:T(8,128)(2,1)}, bf16[128,576]{0,1:T(8,128)(2,1)}, u32[]{:S(2)}, u32[]{:S(2)}) collective-permute-start(bf16[128,576]{0,1:T(8,128)(2,1)} %get-tuple-element.16), channel_id=1, source_target_pairs={{32,0},{40,8},{48,16},{56,24},{64,32},{72,40},{80,48},{88,56},{96,... | collective-permute-start | bytes 442376 | tf_op jit(solution)/shard_map/ppermute | solution.py:18
  166.1 32.0 %collective-permute-start.10 = (bf16[128,576]{0,1:T(8,128)(2,1)}, bf16[128,576]{0,1:T(8,128)(2,1)}, u32[]{:S(2)}, u32[]{:S(2)}) collective-permute-start(bf16[128,576]{0,1:T(8,128)(2,1)} %get-tuple-element.17), channel_id=1, source_target_pairs={{24,0},{32,8},{40,16},{48,24},{56,32},{64,40},{72,48},{80,56},{88,... | collective-permute-start | bytes 442376 | tf_op jit(solution)/shard_map/ppermute | solution.py:18
  167.4 30.7 %collective-permute-start.9 = (bf16[128,576]{0,1:T(8,128)(2,1)}, bf16[128,576]{0,1:T(8,128)(2,1)}, u32[]{:S(2)}, u32[]{:S(2)}) collective-permute-start(bf16[128,576]{0,1:T(8,128)(2,1)} %get-tuple-element.18), channel_id=1, source_target_pairs={{16,0},{24,8},{32,16},{40,24},{48,32},{56,40},{64,48},{72,56},{80,... | collective-permute-start | bytes 442376 | tf_op jit(solution)/shard_map/ppermute | solution.py:18
  187.6 3.3 %copy-start.2 = (bf16[512,2048]{0,1:T(8,128)(2,1)S(1)}, bf16[512,2048]{0,1:T(8,128)(2,1)}, u32[]{:S(2)}) copy-start(bf16[512,2048]{0,1:T(8,128)(2,1)} %copy.66) | copy-start | bytes 6291460
  187.6 3.3 %copy-start.3 = (bf16[128,16,512]{2,0,1:T(8,128)(2,1)S(1)}, bf16[128,16,512]{2,0,1:T(8,128)(2,1)}, u32[]{:S(2)}) copy-start(bf16[128,16,512]{2,0,1:T(8,128)(2,1)} %fusion.29) | copy-start | bytes 6291460
  187.7 4.0 %copy-start.7 = (f32[128,16,64]{0,2,1:T(8,128)S(1)}, f32[128,16,64]{0,2,1:T(8,128)}, u32[]{:S(2)}) copy-start(f32[128,16,64]{0,2,1:T(8,128)} %fusion.14) | copy-start | bytes 1572868
Sparse Core Ops, SparseCore 0:
  116.7 112.4 reduce-scatter.1
Sparse Core Ops, SparseCore 1:
  200.1 85.3 all-reduce.1
where the time goes:
time: 296 us; the launch traced here: 295 us
  matrix products  117 us (40%)
  waiting for transfers between devices  85.5 us (29%)
  starting transfers between devices  32.4 us (11%)
  local copies, waits for them, and re-layouts  32.1 us (11%)
  between operations  15.8 us (5%)
  other arithmetic  12.1 us (4%)
    psum x1, waiting for transfers between devices, body(): grad_total = lax.psum(grad_total, 'head')  54.6 us
    ppermute x12, starting transfers between devices, passed_along(): return lax.ppermute(x, axis, pairs)  32.4 us
    reduce_scatter x1, waiting for transfers between devices, body(): lax.psum_scatter(wgt_terms, 'ctx', scatter_dimension=0, tiled=True)  29.1 us
    dot_general x1, matrix products, attend(): jnp.einsum('thu,thl->ul', grad_scores, absorbed, preferred_element_type=f32)  19.7 us
    dot_general x1, matrix products, attend(): jnp.einsum('thu,ur->thr', grad_scores, k_rope, preferred_element_type=f32)  18.9 us
    dot_general x1, matrix products, attend(): jnp.einsum('thu,thr->ur', grad_scores, q_rope, preferred_element_type=f32)  18.9 us
    dot_general x1, matrix products, attend(): jnp.einsum('thu,ul->thl', grad_scores, c_nope, preferred_element_type=f32)  15 us
    unnamed x33, local copies, waits for them, and re-layouts  12.6 us
  transfers between devices with their start and end apart: 14, of which 4 were waited for; matrix products, arithmetic and copies ran while one was open for 32% of the time, Pallas kernels for 0%

commit v1 on v0

v1 whole, which is shorter than its diff:
```python
import functools

import jax
import jax.numpy as jnp
from jax import lax
from jax.experimental import pallas as pl
from jax.experimental.pallas import tpu as pltpu
from jax.sharding import PartitionSpec as P

LATENT = 512
ROPE = 64
NOPE = 128
WIDE = LATENT + ROPE
QDIM = NOPE + ROPE
SPAN = 4
TOK = 128
HALF = 64
BACK = 448
WINDOW = BACK + TOK
SEEN = BACK + HALF
PACKED = 640
N_CTX = 32
CHUNK = LATENT // N_CTX
HIDDEN = -1e30

bf16 = jnp.bfloat16
f32 = jnp.float32


def dot(a, b, ca=1, cb=0):
    return lax.dot_general(a, b, (((ca,), (cb,)), ((), ())), preferred_element_type=f32)


def place(i):
    return i // 8, (i // 2) % 4, i % 2


def index_of(y, x, c):
    return (y * 4 + x) * 2 + c


NEAR = {0: 1, 1: 0, 2: 3, 3: 2}
FAR = {0: 3, 3: 0, 1: 2, 2: 1}


def halving_pairs(stream):
    order = (NEAR, FAR) if stream == 0 else (FAR, NEAR)
    stages = [[(i, i ^ 1) for i in range(N_CTX)]]
    for turn in (0, 1):
        for step in order:
            pairs = []
            for i in range(N_CTX):
                y, x, c = place(i)
                if c == turn:
                    pairs.append((i, index_of(y, step[x], c)))
                else:
                    pairs.append((i, index_of(step[y], x, c)))
            stages.append(pairs)
    return stages


def chunk_place(me, owner, stream):
    my, mx, mc = me // 8, (me // 2) % 4, me % 2
    oy, ox, oc = place(owner)

    def bits(mine, theirs):
        g = mine ^ (mine >> 1)
        o = theirs ^ (theirs >> 1)
        same = 3 - (g ^ o)
        low, high = same & 1, same >> 1
        return (low, high) if stream == 0 else (high, low)

    xa, xb = bits(mx, ox)
    ya, yb = bits(my, oy)
    first, second = ((xa, xb), (ya, yb)) if oc == 0 else ((ya, yb), (xa, xb))
    same_core = 1 - (mc ^ oc)
    return same_core * 16 + first[0] * 8 + first[1] * 4 + second[0] * 2 + second[1]


def attend_kernel(heads, stream, last, *refs):
    place_ref, q_ref, do_ref, wk_ref, wv_ref, c4, c3, c2, c1, c0 = refs[:10]
    refs = refs[10:]
    if last:
        dcin_ref, refs = refs[0], refs[1:]
        out_ref, gq_ref, dw_ref, own_ref, p1_ref, p2_ref, p3_ref, p4_ref = refs[:8]
        refs = refs[8:]
    else:
        out_ref, gq_ref, dw_ref, dc_ref = refs[:4]
        refs = refs[4:]
    win, ct, absorbed, grad_lat, attended, grad_abs, grad_rope, acc = refs
    scale = QDIM ** -0.5

    win[0:64] = c4[...]
    for n, c in enumerate((c3, c2, c1, c0)):
        win[64 + 128 * n : 192 + 128 * n] = c[...]
    for half in range(2):
        ct[half] = win[half * HALF : half * HALF + SEEN].T

    for h in range(heads):
        q_n = q_ref[:, h * QDIM : h * QDIM + NOPE]
        q_r = q_ref[:, h * QDIM + NOPE : (h + 1) * QDIM]
        cols = slice(h * NOPE, (h + 1) * NOPE)
        a = dot(q_n, wk_ref[:, cols], 1, 1).astype(bf16)
        g = dot(do_ref[:, cols], wv_ref[:, cols], 1, 1).astype(bf16)
        for half in range(2):
            rows = slice(half * HALF, (half + 1) * HALF)
            to = slice(h * HALF, (h + 1) * HALF)
            absorbed[half, to, :LATENT] = a[rows]
            absorbed[half, to, LATENT:WIDE] = q_r[rows]
            grad_lat[half, to] = g[rows]

    if last:
        acc[...] = dcin_ref[...]
    else:
        acc[...] = jnp.zeros_like(acc)

    own = c0[:, WIDE:PACKED].astype(f32)
    query_ids = own[:, 0:1] * 128.0 + own[:, 1:2]
    for half in range(2):
        rows = slice(half * HALF, (half + 1) * HALF)
        keys = slice(half * HALF, half * HALF + SEEN)
        id_rows = ct[half, WIDE : WIDE + 16].astype(f32)
        key_ids = id_rows[0:1] * 128.0 + id_rows[1:2]
        j = lax.broadcasted_iota(jnp.int32, (HALF, SEEN), 1)
        t = lax.broadcasted_iota(jnp.int32, (HALF, SEEN), 0)
        visible = (key_ids == query_ids[rows]) & (j - BACK <= t)
        bias = jnp.where(visible, 0.0, HIDDEN)

        a = absorbed[half][:, :WIDE]
        g = grad_lat[half]
        s = dot(a, ct[half][:WIDE]).reshape(heads, HALF, SEEN) * scale + bias[None]
        s = jnp.exp(s - jnp.max(s, axis=-1, keepdims=True))
        p = s * (1.0 / jnp.sum(s, axis=-1, keepdims=True))
        p_bf = p.astype(bf16).reshape(heads * HALF, SEEN)
        dp = dot(g, ct[half][:LATENT]).reshape(heads, HALF, SEEN)
        delta = jnp.sum(p * dp, axis=-1, keepdims=True)
        ds = (p * (dp - delta) * scale).astype(bf16).reshape(heads * HALF, SEEN)
        att = dot(p_bf, win[keys, :LATENT]).astype(bf16)
        ga = dot(ds, win[keys, :WIDE])
        ga_bf = ga[:, :LATENT].astype(bf16)
        for h in range(heads):
            of = slice(h * HALF, (h + 1) * HALF)
            attended[h, rows] = att[of]
            grad_abs[h, rows] = ga_bf[of]
            grad_rope[h, rows] = ga[of, LATENT:WIDE]
        acc[keys, :LATENT] += dot(p_bf, g, 0, 0)
        acc[keys] += dot(ds, a, 0, 0)

    spots = [pl.multiple_of(place_ref[o] * CHUNK, CHUNK) for o in range(N_CTX)]
    for h in range(heads):
        cols = slice(h * NOPE, (h + 1) * NOPE)
        att = attended[h]
        ga = grad_abs[h]
        out_ref[:, cols] = dot(att, wv_ref[:, cols]).astype(bf16)
        gq_ref[:, h * QDIM : h * QDIM + NOPE] = dot(ga, wk_ref[:, cols])
        gq_ref[:, h * QDIM + NOPE : (h + 1) * QDIM] = grad_rope[h]
        dwk = dot(ga, q_ref[:, h * QDIM : h * QDIM + NOPE], 0, 0).astype(bf16)
        dwv = dot(att, do_ref[:, cols], 0, 0).astype(bf16)
        wv_cols = slice((heads + h) * NOPE, (heads + h + 1) * NOPE)
        for o in range(N_CTX):
            dw_ref[pl.ds(spots[o], CHUNK), cols] = dwk[o * CHUNK : (o + 1) * CHUNK]
            dw_ref[pl.ds(spots[o], CHUNK), wv_cols] = dwv[o * CHUNK : (o + 1) * CHUNK]

    if last:
        p4_ref[...] = acc[0:64].astype(bf16)
        p3_ref[...] = acc[64:192].astype(bf16)
        p2_ref[...] = acc[192:320].astype(bf16)
        p1_ref[...] = acc[320:448].astype(bf16)
        own_ref[...] = acc[448:576]
    else:
        dc_ref[...] = acc[...]


def attend(group, groups, heads, places, blocks, queries, out_grad, w_uk, w_uv, so_far):
    last = group == groups - 1
    whole = lambda shape: pl.BlockSpec(shape, lambda i: (0,) * len(shape))
    part = lambda rows, width: pl.BlockSpec((rows, width), lambda i: (0, group))
    in_specs = [
        pl.BlockSpec(memory_space=pltpu.SMEM),
        part(TOK, heads * QDIM),
        part(TOK, heads * NOPE),
        part(LATENT, heads * NOPE),
        part(LATENT, heads * NOPE),
        whole((HALF, PACKED)),
    ] + [whole((TOK, PACKED))] * 4
    args = [places, queries, out_grad, w_uk, w_uv] + blocks
    shapes = [
        jax.ShapeDtypeStruct((TOK, heads * NOPE), bf16),
        jax.ShapeDtypeStruct((TOK, heads * QDIM), f32),
        jax.ShapeDtypeStruct((LATENT, 2 * heads * NOPE), bf16),
    ]
    if last:
        in_specs.append(whole((WINDOW, WIDE)))
        args.append(so_far)
        shapes += [jax.ShapeDtypeStruct((TOK, WIDE), f32)]
        shapes += [jax.ShapeDtypeStruct((TOK, WIDE), bf16)] * 3
        shapes += [jax.ShapeDtypeStruct((HALF, WIDE), bf16)]
    else:
        shapes += [jax.ShapeDtypeStruct((WINDOW, WIDE), f32)]
    rows = heads * HALF
    return pl.pallas_call(
        functools.partial(attend_kernel, heads, group % 2, last),
        grid=(1,),
        in_specs=in_specs,
        out_specs=[whole(s.shape) for s in shapes],
        out_shape=shapes,
        scratch_shapes=[
            pltpu.VMEM((WINDOW, PACKED), bf16),
            pltpu.VMEM((2, PACKED, SEEN), bf16),
            pltpu.VMEM((2, rows, PACKED), bf16),
            pltpu.VMEM((2, rows, LATENT), bf16),
            pltpu.VMEM((heads, TOK, LATENT), bf16),
            pltpu.VMEM((heads, TOK, LATENT), bf16),
            pltpu.VMEM((heads, TOK, ROPE), f32),
            pltpu.VMEM((WINDOW, WIDE), f32),
        ],
        compiler_params=pltpu.CompilerParams(vmem_limit_bytes=52 * 2**20),
        cost_estimate=pl.CostEstimate(
            flops=int(2 * 2.1e9), bytes_accessed=8 * 2**20, transcendentals=rows * 2 * SEEN
        ),
    )(*args)


def passed_along(x, by):
    pairs = [(i, i + by) for i in range(N_CTX) if 0 <= i + by < N_CTX]
    return lax.ppermute(x, "ctx", pairs)


def halve(x, stream):
    stages = halving_pairs(stream)
    for n, pairs in enumerate(stages):
        h = x.shape[0] // 2
        got = lax.ppermute(x[:h], "ctx", pairs)
        x = x[h:].astype(f32) + got.astype(f32)
        if n < len(stages) - 1:
            x = x.astype(bf16)
    return x


def sum_over_head(x):
    me = lax.axis_index("head")
    odd = (me & 1) == 1
    low, high = x[:HALF], x[HALF:]
    swap = lambda y, d: lax.ppermute(y, "head", [(i, i ^ d) for i in range(8)])
    got = swap(jnp.where(odd, low, high).astype(bf16), 1)
    mine = jnp.where(odd, high, low) + got.astype(f32)
    for d in (2, 4):
        mine = mine.astype(bf16)
        mine = mine.astype(f32) + swap(mine, d).astype(f32)
    mine = mine.astype(bf16)
    other = swap(mine, 1)
    mine, other = mine.astype(f32), other.astype(f32)
    return jnp.concatenate([jnp.where(odd, other, mine), jnp.where(odd, mine, other)], axis=0)


def body(queries, latents, w_uk, w_uv, out_grad, doc_ids):
    ctx = lax.axis_index("ctx")
    groups, heads = 2, 8
    number = doc_ids + 1
    packed = jnp.concatenate(
        [
            latents,
            (number // 128).astype(bf16)[:, None],
            (number % 128).astype(bf16)[:, None],
            jnp.zeros((TOK, PACKED - WIDE - 2), bf16),
        ],
        axis=1,
    )
    blocks = [passed_along(packed[HALF:], 4)]
    blocks += [passed_along(packed, d) for d in (3, 2, 1)] + [packed]
    outs, gqs, weights = [], [], []
    so_far = None
    for group in range(groups):
        places = jnp.stack([chunk_place(ctx, o, group % 2) for o in range(N_CTX)]).astype(jnp.int32)
        res = attend(group, groups, heads, places, blocks, queries, out_grad, w_uk, w_uv, so_far)
        outs.append(res[0])
        gqs.append(res[1])
        weights.append(halve(res[2], group % 2))
        so_far = res[3]
    total, p1, p2, p3, p4 = res[3:]
    for d, piece in ((1, p1), (2, p2), (3, p3)):
        total = total + passed_along(piece, -d).astype(f32)
    far = passed_along(p4, -4).astype(f32)
    total = total + jnp.concatenate([jnp.zeros_like(far), far], axis=0)
    total = sum_over_head(total)
    cut = heads * NOPE
    return (
        jnp.concatenate(outs, axis=1),
        jnp.concatenate(gqs, axis=1),
        total,
        jnp.concatenate([w[:, :cut] for w in weights], axis=1),
        jnp.concatenate([w[:, cut:] for w in weights], axis=1),
    )


def solution(mesh):
    placed = (
        P("ctx", "head"),
        P("ctx", None),
        P(None, "head"),
        P(None, "head"),
        P("ctx", "head"),
        P("ctx"),
    )
    return jax.shard_map(
        body,
        mesh=mesh,
        in_specs=placed,
        out_specs=(
            P("ctx", "head"),
            P("ctx", "head"),
            P("ctx", None),
            P("ctx", "head"),
            P("ctx", "head"),
        ),
        check_vma=False,
    )
```

time: 296 us -> 119 us (0.40)
  matrix products: 117 us -> 0 us
  waiting for transfers between devices: 85.5 us -> 31.9 us
  local copies, waits for them, and re-layouts: 32.1 us -> 6.87 us
  Pallas kernels: 0 us -> 20.8 us
  starting transfers between devices: 32.4 us -> 50.2 us
  between operations: 15.8 us -> 1.26 us
  other arithmetic: 12.1 us -> 6.22 us
    dot_general x14 -> x0, matrix products: 107 us -> none  [the longest x1 19.7 us: attend(): jnp.einsum('thu,thl->ul', grad_scores, absorbed, preferred_element_type=f32)]
    psum x1 -> x0, waiting for transfers between devices: 54.6 us -> none  [body(): grad_total = lax.psum(grad_total, 'head')]
    ppermute x12 -> x22, waiting for transfers between devices: 1.7 us -> 31.9 us  [the longest x10 12 us: halve(): got = lax.ppermute(x[:h], 'ctx', pairs)]
    reduce_scatter x1 -> x0, waiting for transfers between devices: 29.1 us -> none  [body(): lax.psum_scatter(wgt_terms, 'ctx', scatter_dimension=0, tiled=True)]
    pallas_call x0 -> x2, Pallas kernels: none -> 20.8 us  [attend(): pl.pallas_call(functools.partial(attend_kernel, heads, group % 2, last),...]
    ppermute x12 -> x22, starting transfers between devices: 32.4 us -> 50.2 us  [the longest x10 19.9 us: halve(): got = lax.ppermute(x[:h], 'ctx', pairs)]
    reshape x4 -> x0, local copies, waits for them, and re-layouts: 16 us -> none  [the longest x2 10.8 us: body(): wgt_terms = jnp.concatenate([jnp.einsum('thl,thd->lhd', grad_absorbed, q_...]
    unnamed x33 -> x12, local copies, waits for them, and re-layouts: 12.6 us -> 2.98 us
  transfers between devices with their start and end apart: 14 -> 22, of which waited for: 4 -> 12; matrix products, arithmetic and copies ran while one was open for 32% -> 8% of each run, Pallas kernels for 0% -> 0%
where the time goes in v1:
time: 119 us; the launch traced here: 117 us
  starting transfers between devices  50.2 us (42%)
  waiting for transfers between devices  31.9 us (27%)
  Pallas kernels  20.8 us (17%)
  local copies, waits for them, and re-layouts  6.87 us (6%)
  other arithmetic  6.22 us (5%)
  between operations  1.26 us (1%)
    pallas_call x2, Pallas kernels, attend(): pl.pallas_call(functools.partial(attend_kernel, heads, group % 2, last),...  20.8 us
    ppermute x10, starting transfers between devices, halve(): got = lax.ppermute(x[:h], 'ctx', pairs)  19.9 us
    ppermute x8, starting transfers between devices, passed_along(): return lax.ppermute(x, 'ctx', pairs)  19.4 us
    ppermute x10, waiting for transfers between devices, halve(): got = lax.ppermute(x[:h], 'ctx', pairs)  12 us
    ppermute x8, waiting for transfers between devices, passed_along(): return lax.ppermute(x, 'ctx', pairs)  11 us
    ppermute x4, starting transfers between devices, sum_over_head(): swap = lambda y, d: lax.ppermute(y, 'head', [(i, i ^ d) for i in range(8)])  10.8 us
    ppermute x4, waiting for transfers between devices, sum_over_head(): swap = lambda y, d: lax.ppermute(y, 'head', [(i, i ^ d) for i in range(8)])  8.91 us
    slice x10, local copies, waits for them, and re-layouts, halve(): got = lax.ppermute(x[:h], 'ctx', pairs)  3.28 us
  transfers between devices with their start and end apart: 22, of which 12 were waited for; matrix products, arithmetic and copies ran while one was open for 8% of the time, Pallas kernels for 0%

profile of v1, /device:TPU:32, one launch (start us, length us, event | category | flops | bytes accessed | tf_op | source)
XLA Modules:
  0.0 117.3 jit_solution(9409947507024258813)
XLA Ops:
  0.6 0.7 convert_bitcast_fusion
  1.3 0.1 copy.13
  1.4 0.1 copy.12
  1.6 1.1 copy.11
  2.7 0.1 pad.15.clone
  2.7 0.1 maximum_maximum_fusion.refs_9_
  2.8 1.7 %collective-permute-start.3 = (bf16[128,640]{1,0:T(8,128)(2,1)S(1)}, bf16[128,640]{1,0:T(8,128)(2,1)S(1)}, u32[]{:S(2)}, u32[]{:S(2)}) collective-permute-start(bf16[128,640]{1,0:T(8,128)(2,1)S(1)} %maximum_maximum_fusion.refs_9_), channel_id=1, source_target_pairs={{0,8},{8,16},{16,24},{24,32},{32,40},{40,48},{48,56},{56,64},{64,7... | collective-permute-start | bytes 491528 | tf_op jit(solution)/shard_map/ppermute | solution.py:226
  4.6 3.6 %collective-permute-start.2 = (bf16[128,640]{1,0:T(8,128)(2,1)S(1)}, bf16[128,640]{1,0:T(8,128)(2,1)S(1)}, u32[]{:S(2)}, u32[]{:S(2)}) collective-permute-start(bf16[128,640]{1,0:T(8,128)(2,1)S(1)} %maximum_maximum_fusion.refs_9_), channel_id=1, source_target_pairs={{0,16},{8,24},{16,32},{24,40},{32,48},{40,56},{48,64},{56,72},{64,... | collective-permute-start | bytes 491528 | tf_op jit(solution)/shard_map/ppermute | solution.py:226
  8.2 4.0 %collective-permute-start.1 = (bf16[128,640]{1,0:T(8,128)(2,1)S(1)}, bf16[128,640]{1,0:T(8,128)(2,1)S(1)}, u32[]{:S(2)}, u32[]{:S(2)}) collective-permute-start(bf16[128,640]{1,0:T(8,128)(2,1)S(1)} %maximum_maximum_fusion.refs_9_), channel_id=1, source_target_pairs={{0,24},{8,32},{16,40},{24,48},{32,56},{40,64},{48,72},{56,80},{64,... | collective-permute-start | bytes 491528 | tf_op jit(solution)/shard_map/ppermute | solution.py:226
  12.2 4.9 %collective-permute-start = (bf16[64,640]{1,0:T(8,128)(2,1)S(1)}, bf16[64,640]{1,0:T(8,128)(2,1)S(1)}, u32[]{:S(2)}, u32[]{:S(2)}) collective-permute-start(bf16[64,640]{1,0:T(8,128)(2,1)S(1)} %slice.108), channel_id=1, source_target_pairs={{0,32},{8,40},{16,48},{24,56},{32,64},{40,72},{48,80},{56,88},{64,... | collective-permute-start | bytes 245768 | tf_op jit(solution)/shard_map/ppermute | solution.py:226
  17.4 0.1 stack.230.refs_0_
  17.6 0.1 stack.263.refs_0_
  17.7 1.5 %collective-permute-done.refs_5_ = bf16[64,640]{1,0:T(8,128)(2,1)S(1)} collective-permute-done((bf16[64,640]{1,0:T(8,128)(2,1)S(1)}, bf16[64,640]{1,0:T(8,128)(2,1)S(1)}, u32[]{:S(2)}, u32[]{:S(2)}) %collective-permute-start) | collective-permute-done | bytes 81952 | tf_op jit(solution)/shard_map/ppermute | solution.py:226
  19.2 0.0 collective-permute-done.3.refs_8_
  19.2 0.0 collective-permute-done.2.refs_7_
  19.2 0.0 collective-permute-done.1.refs_6_
  19.2 0.0 copy-start
  19.2 1.0 copy-done
  20.2 10.3 %shard_map.101 = (bf16[128,1024]{1,0:T(8,128)(2,1)S(1)}, f32[128,1536]{1,0:T(8,128)}, bf16[512,2048]{1,0:T(8,128)(2,1)}, f32[576,576]{1,0:T(8,128)}) custom-call(s32[32]{0:T(128)S(1)} %stack.230.refs_0_, bf16[128,3072]{1,0:T(8,128)(2,1)} %refs_1_.3, bf16[128,2048]{1,0:T(8,128)(2,1)S(1)} %copy-done, bf16[512,2048]{1,0:T(8,128)(2,1)} %refs_3_.3, ...), custom_call_target="tpu_custom_call" | custom-call | flops 4200000000 | bytes 8388608 | tf_op jit(solution)/shard_map/pallas_call | solution.py:201
  30.5 10.5 %shard_map.102 = (bf16[128,1024]{1,0:T(8,128)(2,1)S(1)}, f32[128,1536]{1,0:T(8,128)}, bf16[512,2048]{1,0:T(8,128)(2,1)}, f32[128,576]{1,0:T(8,128)S(1)}, bf16[12...) custom-call(s32[32]{0:T(128)S(1)} %stack.263.refs_0_, ...), custom_call_target="tpu_custom_call" | custom-call | flops 4200000000 | bytes 8388608 | tf_op jit(solution)/shard_map/pallas_call | solution.py:201
  41.1 1.3 %collective-permute-start.4 = (bf16[128,576]{1,0:T(8,128)(2,1)S(1)}, bf16[128,576]{1,0:T(8,128)(2,1)S(1)}, u32[]{:S(2)}, u32[]{:S(2)}) collective-permute-start(bf16[128,576]{1,0:T(8,128)(2,1)S(1)} %get-tuple-element.23), channel_id=1, source_target_pairs={{8,0},{16,8},{24,16},{32,24},{40,32},{48,40},{56,48},{64,56},{72,6... | collective-permute-start | bytes 442376 | tf_op jit(solution)/shard_map/ppermute | solution.py:226
  42.4 1.3 %collective-permute-start.5 = (bf16[128,576]{1,0:T(8,128)(2,1)S(1)}, bf16[128,576]{1,0:T(8,128)(2,1)S(1)}, u32[]{:S(2)}, u32[]{:S(2)}) collective-permute-start(bf16[128,576]{1,0:T(8,128)(2,1)S(1)} %get-tuple-element.24), channel_id=1, source_target_pairs={{16,0},{24,8},{32,16},{40,24},{48,32},{56,40},{64,48},{72,56},{80,... | collective-permute-start | bytes 442376 | tf_op jit(solution)/shard_map/ppermute | solution.py:226
  43.7 1.3 %collective-permute-start.6 = (bf16[128,576]{1,0:T(8,128)(2,1)S(1)}, bf16[128,576]{1,0:T(8,128)(2,1)S(1)}, u32[]{:S(2)}, u32[]{:S(2)}) collective-permute-start(bf16[128,576]{1,0:T(8,128)(2,1)S(1)} %get-tuple-element.25), channel_id=1, source_target_pairs={{24,0},{32,8},{40,16},{48,24},{56,32},{64,40},{72,48},{80,56},{88,... | collective-permute-start | bytes 442376 | tf_op jit(solution)/shard_map/ppermute | solution.py:226
  45.0 1.3 %collective-permute-start.7 = (bf16[64,576]{1,0:T(8,128)(2,1)S(1)}, bf16[64,576]{1,0:T(8,128)(2,1)S(1)}, u32[]{:S(2)}, u32[]{:S(2)}) collective-permute-start(bf16[64,576]{1,0:T(8,128)(2,1)S(1)} %get-tuple-element.26), channel_id=1, source_target_pairs={{32,0},{40,8},{48,16},{56,24},{64,32},{72,40},{80,48},{88,56},{96,... | collective-permute-start | bytes 221192 | tf_op jit(solution)/shard_map/ppermute | solution.py:226
  46.3 9.5 %collective-permute-done.7 = bf16[64,576]{1,0:T(8,128)(2,1)S(1)} collective-permute-done((bf16[64,576]{1,0:T(8,128)(2,1)S(1)}, bf16[64,576]{1,0:T(8,128)(2,1)S(1)}, u32[]{:S(2)}, u32[]{:S(2)}) %collective-permute-start.7) | collective-permute-done | bytes 73760 | tf_op jit(solution)/shard_map/ppermute | solution.py:226
  55.8 0.1 convert_add_fusion
  55.9 0.2 collective-permute-start.8
  56.1 4.3 %collective-permute-done.8 = bf16[64,576]{1,0:T(8,128)(2,1)S(1)} collective-permute-done((bf16[64,576]{1,0:T(8,128)(2,1)S(1)}, bf16[64,576]{1,0:T(8,128)(2,1)S(1)}, u32[]{:S(2)}, u32[]{:S(2)}) %collective-permute-start.8) | collective-permute-done | bytes 73760 | tf_op jit(solution)/shard_map/ppermute | solution.py:244
  60.4 3.4 %collective-permute-start.9 = (bf16[64,576]{1,0:T(8,128)(2,1)S(1)}, bf16[64,576]{1,0:T(8,128)(2,1)S(1)}, u32[]{:S(2)}, u32[]{:S(2)}) collective-permute-start(bf16[64,576]{1,0:T(8,128)(2,1)S(1)} %add_convert_fusion.10), channel_id=1, source_target_pairs={{0,2},{1,3},{2,0},{3,1},{4,6},{5,7},{6,4},{7,5},{8,10},{9,11},{10,... | collective-permute-start | bytes 221192 | tf_op jit(solution)/shard_map/ppermute | solution.py:244
  63.8 1.4 %slice.85 = bf16[256,2048]{1,0:T(8,128)(2,1)S(1)} slice(bf16[512,2048]{1,0:T(8,128)(2,1)} %get-tuple-element.27), slice={[0:256], [0:2048]} | slice | bytes 2097152 | tf_op jit(solution)/shard_map/slice | solution.py:233
  65.3 0.1 collective-permute-start.12
  65.4 0.1 slice.96
  65.5 0.6 collective-permute-start.17
  66.1 0.2 collective-permute-done.9
  66.3 6.1 %collective-permute-start.10 = (bf16[64,576]{1,0:T(8,128)(2,1)S(1)}, bf16[64,576]{1,0:T(8,128)(2,1)S(1)}, u32[]{:S(2)}, u32[]{:S(2)}) collective-permute-start(bf16[64,576]{1,0:T(8,128)(2,1)S(1)} %add_convert_fusion.9), channel_id=1, source_target_pairs={{0,4},{1,5},{2,6},{3,7},{4,0},{5,1},{6,2},{7,3},{8,12},{9,13},{10,... | collective-permute-start | bytes 221192 | tf_op jit(solution)/shard_map/ppermute | solution.py:244
  72.4 1.3 %pad_maximum_fusion = f32[128,3072]{1,0:T(8,128)} fusion(f32[128,1536]{1,0:T(8,128)S(1)} %copy-done.4, f32[128,1536]{1,0:T(8,128)S(1)} %copy-done.3), kind=kLoop, calls=%fused_computation.2 | loop fusion | flops 393216 | bytes 3145728 | tf_op jit(solution)/shard_map/concatenate | solution.py:289
  73.6 1.9 %collective-permute-done.10 = bf16[64,576]{1,0:T(8,128)(2,1)S(1)} collective-permute-done((bf16[64,576]{1,0:T(8,128)(2,1)S(1)}, bf16[64,576]{1,0:T(8,128)(2,1)S(1)}, u32[]{:S(2)}, u32[]{:S(2)}) %collective-permute-start.10) | collective-permute-done | bytes 73760 | tf_op jit(solution)/shard_map/ppermute | solution.py:244
  75.5 1.2 collective-permute-start.11
  76.7 0.8 pad_maximum_fusion.1
  77.5 2.5 %collective-permute-done.11 = bf16[64,576]{1,0:T(8,128)(2,1)S(1)} collective-permute-done((bf16[64,576]{1,0:T(8,128)(2,1)S(1)}, bf16[64,576]{1,0:T(8,128)(2,1)S(1)}, u32[]{:S(2)}, u32[]{:S(2)}) %collective-permute-start.11) | collective-permute-done | bytes 73760 | tf_op jit(solution)/shard_map/ppermute | solution.py:244
  80.1 0.5 add_convert_fusion.1
  80.6 0.8 slice.112
  81.4 4.1 %collective-permute-start.13 = (bf16[128,2048]{1,0:T(8,128)(2,1)}, bf16[128,2048]{1,0:T(8,128)(2,1)S(1)}, u32[]{:S(2)}, u32[]{:S(2)}) collective-permute-start(bf16[128,2048]{1,0:T(8,128)(2,1)} %slice.112), channel_id=1, source_target_pairs={{0,16},{8,72},{16,0},{24,88},{32,48},{40,104},{48,32},{56,120},{64... | collective-permute-start | bytes 1572872 | tf_op jit(solution)/shard_map/ppermute | solution.py:233
  85.5 0.5 add_convert_fusion
  86.0 0.8 slice.121
  86.8 2.9 %collective-permute-start.18 = (bf16[128,2048]{1,0:T(8,128)(2,1)}, bf16[128,2048]{1,0:T(8,128)(2,1)}, u32[]{:S(2)}, u32[]{:S(2)}) collective-permute-start(bf16[128,2048]{1,0:T(8,128)(2,1)} %slice.121), channel_id=1, source_target_pairs={{0,48},{8,200},{16,32},{24,216},{32,16},{40,232},{48,0},{56,248},{... | collective-permute-start | bytes 1572872 | tf_op jit(solution)/shard_map/ppermute | solution.py:233
  89.8 0.9 copy.14
  90.6 2.2 %collective-permute-done.13 = bf16[128,2048]{1,0:T(8,128)(2,1)S(1)} collective-permute-done((bf16[128,2048]{1,0:T(8,128)(2,1)}, bf16[128,2048]{1,0:T(8,128)(2,1)S(1)}, u32[]{:S(2)}, u32[]{:S(2)}) %collective-permute-start.13) | collective-permute-done | bytes 524320 | tf_op jit(solution)/shard_map/ppermute | solution.py:233
  92.9 0.1 add_convert_fusion.3
  93.1 5.0 %collective-permute-start.14 = (bf16[64,2048]{1,0:T(8,128)(2,1)S(1)}, bf16[64,2048]{1,0:T(8,128)(2,1)S(1)}, u32[]{:S(2)}, u32[]{:S(2)}) collective-permute-start(bf16[64,2048]{1,0:T(8,128)(2,1)S(1)} %slice.114), channel_id=1, source_target_pairs={{0,48},{8,200},{16,32},{24,216},{32,16},{40,232},{48,0},{56,248},{... | collective-permute-start | bytes 786440 | tf_op jit(solution)/shard_map/ppermute | solution.py:233
  98.1 1.2 add_convert_fusion.2
  99.3 0.6 collective-permute-start.19
  99.9 2.5 %collective-permute-done.14 = bf16[64,2048]{1,0:T(8,128)(2,1)S(1)} collective-permute-done((bf16[64,2048]{1,0:T(8,128)(2,1)S(1)}, bf16[64,2048]{1,0:T(8,128)(2,1)S(1)}, u32[]{:S(2)}, u32[]{:S(2)}) %collective-permute-start.14) | collective-permute-done | bytes 262176 | tf_op jit(solution)/shard_map/ppermute | solution.py:233
  102.4 0.1 add_convert_fusion.5
  102.5 1.5 %collective-permute-start.15 = (bf16[32,2048]{1,0:T(8,128)(2,1)S(1)}, bf16[32,2048]{1,0:T(8,128)(2,1)S(1)}, u32[]{:S(2)}, u32[]{:S(2)}) collective-permute-start(bf16[32,2048]{1,0:T(8,128)(2,1)S(1)} %slice.116), channel_id=1, source_target_pairs={{0,64},{8,24},{16,80},{24,8},{32,96},{40,56},{48,112},{56,40},{64,... | collective-permute-start | bytes 393224 | tf_op jit(solution)/shard_map/ppermute | solution.py:233
  104.1 1.7 %collective-permute-done.19 = bf16[64,2048]{1,0:T(8,128)(2,1)S(1)} collective-permute-done((bf16[64,2048]{1,0:T(8,128)(2,1)S(1)}, bf16[64,2048]{1,0:T(8,128)(2,1)S(1)}, u32[]{:S(2)}, u32[]{:S(2)}) %collective-permute-start.19) | collective-permute-done | bytes 262176 | tf_op jit(solution)/shard_map/ppermute | solution.py:233
  105.8 0.1 add_convert_fusion.4
  105.9 2.9 %collective-permute-start.20 = (bf16[32,2048]{1,0:T(8,128)(2,1)S(1)}, bf16[32,2048]{1,0:T(8,128)(2,1)S(1)}, u32[]{:S(2)}, u32[]{:S(2)}) collective-permute-start(bf16[32,2048]{1,0:T(8,128)(2,1)S(1)} %slice.125), channel_id=1, source_target_pairs={{0,192},{8,56},{16,208},{24,40},{32,224},{40,24},{48,240},{56,8},{... | collective-permute-start | bytes 393224 | tf_op jit(solution)/shard_map/ppermute | solution.py:233
  108.8 1.8 %collective-permute-start.16 = (bf16[16,2048]{1,0:T(8,128)(2,1)S(1)}, bf16[16,2048]{1,0:T(8,128)(2,1)S(1)}, u32[]{:S(2)}, u32[]{:S(2)}) collective-permute-start(bf16[16,2048]{1,0:T(8,128)(2,1)S(1)} %slice.118), channel_id=1, source_target_pairs={{0,192},{8,56},{16,208},{24,40},{32,224},{40,24},{48,240},{56,8},{... | collective-permute-start | bytes 196616 | tf_op jit(solution)/shard_map/ppermute | solution.py:233
  110.6 1.5 %collective-permute-done.20 = bf16[32,2048]{1,0:T(8,128)(2,1)S(1)} collective-permute-done((bf16[32,2048]{1,0:T(8,128)(2,1)S(1)}, bf16[32,2048]{1,0:T(8,128)(2,1)S(1)}, u32[]{:S(2)}, u32[]{:S(2)}) %collective-permute-start.20) | collective-permute-done | bytes 131104 | tf_op jit(solution)/shard_map/ppermute | solution.py:233
  112.2 0.3 collective-permute-start.21
  112.5 1.8 %collective-permute-done.16 = bf16[16,2048]{1,0:T(8,128)(2,1)S(1)} collective-permute-done((bf16[16,2048]{1,0:T(8,128)(2,1)S(1)}, bf16[16,2048]{1,0:T(8,128)(2,1)S(1)}, u32[]{:S(2)}, u32[]{:S(2)}) %collective-permute-start.16) | collective-permute-done | bytes 65568 | tf_op jit(solution)/shard_map/ppermute | solution.py:233
  114.4 2.2 %collective-permute-done.21 = bf16[16,2048]{1,0:T(8,128)(2,1)S(1)} collective-permute-done((bf16[16,2048]{1,0:T(8,128)(2,1)S(1)}, bf16[16,2048]{1,0:T(8,128)(2,1)S(1)}, u32[]{:S(2)}, u32[]{:S(2)}) %collective-permute-start.21) | collective-permute-done | bytes 65568 | tf_op jit(solution)/shard_map/ppermute | solution.py:233
  116.6 0.7 pad_maximum_fusion.3
  (36 shorter events, 0.4 us)
Async XLA Ops:
  2.8 16.4 %collective-permute-start.3 = (bf16[128,640]{1,0:T(8,128)(2,1)S(1)}, bf16[128,640]{1,0:T(8,128)(2,1)S(1)}, u32[]{:S(2)}, u32[]{:S(2)}) collective-permute-start(bf16[128,640]{1,0:T(8,128)(2,1)S(1)} %maximum_maximum_fusion.refs_9_), channel_id=1, source_target_pairs={{0,8},{8,16},{16,24},{24,32},{32,40},{40,48},{48,56},{56,64},{64,7... | collective-permute-start | bytes 491528 | tf_op jit(solution)/shard_map/ppermute | solution.py:226
  4.6 14.6 %collective-permute-start.2 = (bf16[128,640]{1,0:T(8,128)(2,1)S(1)}, bf16[128,640]{1,0:T(8,128)(2,1)S(1)}, u32[]{:S(2)}, u32[]{:S(2)}) collective-permute-start(bf16[128,640]{1,0:T(8,128)(2,1)S(1)} %maximum_maximum_fusion.refs_9_), channel_id=1, source_target_pairs={{0,16},{8,24},{16,32},{24,40},{32,48},{40,56},{48,64},{56,72},{64,... | collective-permute-start | bytes 491528 | tf_op jit(solution)/shard_map/ppermute | solution.py:226
  8.2 11.0 %collective-permute-start.1 = (bf16[128,640]{1,0:T(8,128)(2,1)S(1)}, bf16[128,640]{1,0:T(8,128)(2,1)S(1)}, u32[]{:S(2)}, u32[]{:S(2)}) collective-permute-start(bf16[128,640]{1,0:T(8,128)(2,1)S(1)} %maximum_maximum_fusion.refs_9_), channel_id=1, source_target_pairs={{0,24},{8,32},{16,40},{24,48},{32,56},{40,64},{48,72},{56,80},{64,... | collective-permute-start | bytes 491528 | tf_op jit(solution)/shard_map/ppermute | solution.py:226
  12.2 7.0 %collective-permute-start = (bf16[64,640]{1,0:T(8,128)(2,1)S(1)}, bf16[64,640]{1,0:T(8,128)(2,1)S(1)}, u32[]{:S(2)}, u32[]{:S(2)}) collective-permute-start(bf16[64,640]{1,0:T(8,128)(2,1)S(1)} %slice.108), channel_id=1, source_target_pairs={{0,32},{8,40},{16,48},{24,56},{32,64},{40,72},{48,80},{56,88},{64,... | collective-permute-start | bytes 245768 | tf_op jit(solution)/shard_map/ppermute | solution.py:226
  19.2 1.0 copy-start
  41.1 14.7 %collective-permute-start.4 = (bf16[128,576]{1,0:T(8,128)(2,1)S(1)}, bf16[128,576]{1,0:T(8,128)(2,1)S(1)}, u32[]{:S(2)}, u32[]{:S(2)}) collective-permute-start(bf16[128,576]{1,0:T(8,128)(2,1)S(1)} %get-tuple-element.23), channel_id=1, source_target_pairs={{8,0},{16,8},{24,16},{32,24},{40,32},{48,40},{56,48},{64,56},{72,6... | collective-permute-start | bytes 442376 | tf_op jit(solution)/shard_map/ppermute | solution.py:226
  42.4 13.4 %collective-permute-start.5 = (bf16[128,576]{1,0:T(8,128)(2,1)S(1)}, bf16[128,576]{1,0:T(8,128)(2,1)S(1)}, u32[]{:S(2)}, u32[]{:S(2)}) collective-permute-start(bf16[128,576]{1,0:T(8,128)(2,1)S(1)} %get-tuple-element.24), channel_id=1, source_target_pairs={{16,0},{24,8},{32,16},{40,24},{48,32},{56,40},{64,48},{72,56},{80,... | collective-permute-start | bytes 442376 | tf_op jit(solution)/shard_map/ppermute | solution.py:226
  43.7 12.1 %collective-permute-start.6 = (bf16[128,576]{1,0:T(8,128)(2,1)S(1)}, bf16[128,576]{1,0:T(8,128)(2,1)S(1)}, u32[]{:S(2)}, u32[]{:S(2)}) collective-permute-start(bf16[128,576]{1,0:T(8,128)(2,1)S(1)} %get-tuple-element.25), channel_id=1, source_target_pairs={{24,0},{32,8},{40,16},{48,24},{56,32},{64,40},{72,48},{80,56},{88,... | collective-permute-start | bytes 442376 | tf_op jit(solution)/shard_map/ppermute | solution.py:226
  45.0 10.8 %collective-permute-start.7 = (bf16[64,576]{1,0:T(8,128)(2,1)S(1)}, bf16[64,576]{1,0:T(8,128)(2,1)S(1)}, u32[]{:S(2)}, u32[]{:S(2)}) collective-permute-start(bf16[64,576]{1,0:T(8,128)(2,1)S(1)} %get-tuple-element.26), channel_id=1, source_target_pairs={{32,0},{40,8},{48,16},{56,24},{64,32},{72,40},{80,48},{88,56},{96,... | collective-permute-start | bytes 221192 | tf_op jit(solution)/shard_map/ppermute | solution.py:226
  46.3 19.1 %copy-start.1 = (bf16[512,2048]{1,0:T(8,128)(2,1)S(1)}, bf16[512,2048]{1,0:T(8,128)(2,1)}, u32[]{:S(2)}) copy-start(bf16[512,2048]{1,0:T(8,128)(2,1)} %get-tuple-element.28) | copy-start | bytes 6291460
  55.9 4.5 %collective-permute-start.8 = (bf16[64,576]{1,0:T(8,128)(2,1)S(1)}, bf16[64,576]{1,0:T(8,128)(2,1)S(1)}, u32[]{:S(2)}, u32[]{:S(2)}) collective-permute-start(bf16[64,576]{1,0:T(8,128)(2,1)S(1)} %select_convert_fusion), channel_id=1, source_target_pairs={{0,1},{1,0},{2,3},{3,2},{4,5},{5,4},{6,7},{7,6},{8,9},{9,8},{10,11... | collective-permute-start | bytes 221192 | tf_op jit(solution)/shard_map/ppermute | solution.py:244
  60.4 5.8 %collective-permute-start.9 = (bf16[64,576]{1,0:T(8,128)(2,1)S(1)}, bf16[64,576]{1,0:T(8,128)(2,1)S(1)}, u32[]{:S(2)}, u32[]{:S(2)}) collective-permute-start(bf16[64,576]{1,0:T(8,128)(2,1)S(1)} %add_convert_fusion.10), channel_id=1, source_target_pairs={{0,2},{1,3},{2,0},{3,1},{4,6},{5,7},{6,4},{7,5},{8,10},{9,11},{10,... | collective-permute-start | bytes 221192 | tf_op jit(solution)/shard_map/ppermute | solution.py:244
  63.8 8.5 %copy-start.3 = (f32[128,1536]{1,0:T(8,128)S(1)}, f32[128,1536]{1,0:T(8,128)}, u32[]{:S(2)}) copy-start(f32[128,1536]{1,0:T(8,128)} %get-tuple-element.20) | copy-start | bytes 2359300
  63.8 8.5 %copy-start.4 = (f32[128,1536]{1,0:T(8,128)S(1)}, f32[128,1536]{1,0:T(8,128)}, u32[]{:S(2)}) copy-start(f32[128,1536]{1,0:T(8,128)} %get-tuple-element.21) | copy-start | bytes 2359300
  65.3 14.8 %collective-permute-start.12 = (bf16[256,2048]{1,0:T(8,128)(2,1)S(1)}, bf16[256,2048]{1,0:T(8,128)(2,1)S(1)}, u32[]{:S(2)}, u32[]{:S(2)}) collective-permute-start(bf16[256,2048]{1,0:T(8,128)(2,1)S(1)} %slice.85), channel_id=1, source_target_pairs={{0,8},{8,0},{16,24},{24,16},{32,40},{40,32},{48,56},{56,48},{64,72... | collective-permute-start | bytes 3145736 | tf_op jit(solution)/shard_map/ppermute | solution.py:233
  65.5 20.0 %collective-permute-start.17 = (bf16[256,2048]{1,0:T(8,128)(2,1)S(1)}, bf16[256,2048]{1,0:T(8,128)(2,1)S(1)}, u32[]{:S(2)}, u32[]{:S(2)}) collective-permute-start(bf16[256,2048]{1,0:T(8,128)(2,1)S(1)} %slice.96), channel_id=1, source_target_pairs={{0,8},{8,0},{16,24},{24,16},{32,40},{40,32},{48,56},{56,48},{64,72... | collective-permute-start | bytes 3145736 | tf_op jit(solution)/shard_map/ppermute | solution.py:233
  66.3 9.2 %collective-permute-start.10 = (bf16[64,576]{1,0:T(8,128)(2,1)S(1)}, bf16[64,576]{1,0:T(8,128)(2,1)S(1)}, u32[]{:S(2)}, u32[]{:S(2)}) collective-permute-start(bf16[64,576]{1,0:T(8,128)(2,1)S(1)} %add_convert_fusion.9), channel_id=1, source_target_pairs={{0,4},{1,5},{2,6},{3,7},{4,0},{5,1},{6,2},{7,3},{8,12},{9,13},{10,... | collective-permute-start | bytes 221192 | tf_op jit(solution)/shard_map/ppermute | solution.py:244
  72.4 7.7 %copy-start.2 = (bf16[512,2048]{1,0:T(8,128)(2,1)S(1)}, bf16[512,2048]{1,0:T(8,128)(2,1)}, u32[]{:S(2)}) copy-start(bf16[512,2048]{1,0:T(8,128)(2,1)} %get-tuple-element.27) | copy-start | bytes 6291460
  75.5 4.5 %collective-permute-start.11 = (bf16[64,576]{1,0:T(8,128)(2,1)S(1)}, bf16[64,576]{1,0:T(8,128)(2,1)S(1)}, u32[]{:S(2)}, u32[]{:S(2)}) collective-permute-start(bf16[64,576]{1,0:T(8,128)(2,1)S(1)} %add_convert_fusion.8), channel_id=1, source_target_pairs={{0,1},{1,0},{2,3},{3,2},{4,5},{5,4},{6,7},{7,6},{8,9},{9,8},{10,11... | collective-permute-start | bytes 221192 | tf_op jit(solution)/shard_map/ppermute | solution.py:244
  81.4 11.5 %collective-permute-start.13 = (bf16[128,2048]{1,0:T(8,128)(2,1)}, bf16[128,2048]{1,0:T(8,128)(2,1)S(1)}, u32[]{:S(2)}, u32[]{:S(2)}) collective-permute-start(bf16[128,2048]{1,0:T(8,128)(2,1)} %slice.112), channel_id=1, source_target_pairs={{0,16},{8,72},{16,0},{24,88},{32,48},{40,104},{48,32},{56,120},{64... | collective-permute-start | bytes 1572872 | tf_op jit(solution)/shard_map/ppermute | solution.py:233
  86.8 11.3 %collective-permute-start.18 = (bf16[128,2048]{1,0:T(8,128)(2,1)}, bf16[128,2048]{1,0:T(8,128)(2,1)}, u32[]{:S(2)}, u32[]{:S(2)}) collective-permute-start(bf16[128,2048]{1,0:T(8,128)(2,1)} %slice.121), channel_id=1, source_target_pairs={{0,48},{8,200},{16,32},{24,216},{32,16},{40,232},{48,0},{56,248},{... | collective-permute-start | bytes 1572872 | tf_op jit(solution)/shard_map/ppermute | solution.py:233
  93.1 9.4 %collective-permute-start.14 = (bf16[64,2048]{1,0:T(8,128)(2,1)S(1)}, bf16[64,2048]{1,0:T(8,128)(2,1)S(1)}, u32[]{:S(2)}, u32[]{:S(2)}) collective-permute-start(bf16[64,2048]{1,0:T(8,128)(2,1)S(1)} %slice.114), channel_id=1, source_target_pairs={{0,48},{8,200},{16,32},{24,216},{32,16},{40,232},{48,0},{56,248},{... | collective-permute-start | bytes 786440 | tf_op jit(solution)/shard_map/ppermute | solution.py:233
  99.3 6.5 %collective-permute-start.19 = (bf16[64,2048]{1,0:T(8,128)(2,1)S(1)}, bf16[64,2048]{1,0:T(8,128)(2,1)S(1)}, u32[]{:S(2)}, u32[]{:S(2)}) collective-permute-start(bf16[64,2048]{1,0:T(8,128)(2,1)S(1)} %slice.123), channel_id=1, source_target_pairs={{0,16},{8,72},{16,0},{24,88},{32,48},{40,104},{48,32},{56,120},{64... | collective-permute-start | bytes 786440 | tf_op jit(solution)/shard_map/ppermute | solution.py:233
  102.5 6.2 %collective-permute-start.15 = (bf16[32,2048]{1,0:T(8,128)(2,1)S(1)}, bf16[32,2048]{1,0:T(8,128)(2,1)S(1)}, u32[]{:S(2)}, u32[]{:S(2)}) collective-permute-start(bf16[32,2048]{1,0:T(8,128)(2,1)S(1)} %slice.116), channel_id=1, source_target_pairs={{0,64},{8,24},{16,80},{24,8},{32,96},{40,56},{48,112},{56,40},{64,... | collective-permute-start | bytes 393224 | tf_op jit(solution)/shard_map/ppermute | solution.py:233
  105.9 6.3 %collective-permute-start.20 = (bf16[32,2048]{1,0:T(8,128)(2,1)S(1)}, bf16[32,2048]{1,0:T(8,128)(2,1)S(1)}, u32[]{:S(2)}, u32[]{:S(2)}) collective-permute-start(bf16[32,2048]{1,0:T(8,128)(2,1)S(1)} %slice.125), channel_id=1, source_target_pairs={{0,192},{8,56},{16,208},{24,40},{32,224},{40,24},{48,240},{56,8},{... | collective-permute-start | bytes 393224 | tf_op jit(solution)/shard_map/ppermute | solution.py:233
  108.8 5.6 %collective-permute-start.16 = (bf16[16,2048]{1,0:T(8,128)(2,1)S(1)}, bf16[16,2048]{1,0:T(8,128)(2,1)S(1)}, u32[]{:S(2)}, u32[]{:S(2)}) collective-permute-start(bf16[16,2048]{1,0:T(8,128)(2,1)S(1)} %slice.118), channel_id=1, source_target_pairs={{0,192},{8,56},{16,208},{24,40},{32,224},{40,24},{48,240},{56,8},{... | collective-permute-start | bytes 196616 | tf_op jit(solution)/shard_map/ppermute | solution.py:233
  112.2 4.4 %collective-permute-start.21 = (bf16[16,2048]{1,0:T(8,128)(2,1)S(1)}, bf16[16,2048]{1,0:T(8,128)(2,1)S(1)}, u32[]{:S(2)}, u32[]{:S(2)}) collective-permute-start(bf16[16,2048]{1,0:T(8,128)(2,1)S(1)} %slice.127), channel_id=1, source_target_pairs={{0,64},{8,24},{16,80},{24,8},{32,96},{40,56},{48,112},{56,40},{64,... | collective-permute-start | bytes 196616 | tf_op jit(solution)/shard_map/ppermute | solution.py:233

commit v2 on v1

v2 whole, which is shorter than its diff:
```python
import functools

import jax
import jax.numpy as jnp
from jax import lax
from jax.experimental import pallas as pl
from jax.experimental.pallas import tpu as pltpu
from jax.sharding import PartitionSpec as P

LATENT = 512
ROPE = 64
NOPE = 128
WIDE = LATENT + ROPE
QDIM = NOPE + ROPE
SPAN = 4
TOK = 128
HALF = 64
BACK = 448
WINDOW = BACK + TOK
SEEN = BACK + HALF
PACKED = 640
N_CTX = 32
CHUNK = LATENT // N_CTX
HIDDEN = -1e30

bf16 = jnp.bfloat16
f32 = jnp.float32


def dot(a, b, ca=1, cb=0):
    return lax.dot_general(a, b, (((ca,), (cb,)), ((), ())), preferred_element_type=f32)


def place(i):
    return i // 8, (i // 2) % 4, i % 2


def index_of(y, x, c):
    return (y * 4 + x) * 2 + c


NEAR = {0: 1, 1: 0, 2: 3, 3: 2}
FAR = {0: 3, 3: 0, 1: 2, 2: 1}


def halving_pairs(stream):
    order = (NEAR, FAR) if stream == 0 else (FAR, NEAR)
    stages = []
    for turn, steps in ((0, order), (1, (NEAR, FAR))):
        for step in steps:
            pairs = []
            for i in range(N_CTX):
                y, x, c = place(i)
                if c == turn:
                    pairs.append((i, index_of(y, step[x], c)))
                else:
                    pairs.append((i, index_of(step[y], x, c)))
            stages.append(pairs)
    return stages


def chunk_places(me, stream):
    chips = jnp.arange(16, dtype=jnp.int32)
    my, mx, mc = me // 8, (me // 2) % 4, me % 2

    def bits(mine, theirs):
        same = 3 - ((mine ^ (mine >> 1)) ^ (theirs ^ (theirs >> 1)))
        return same & 1, same >> 1

    (xl, xh), (yl, yh) = bits(mx, chips % 4), bits(my, chips // 4)
    if stream == 0:
        x_first = xl * 8 + xh * 4 + yl * 2 + yh
        y_first = yl * 8 + yh * 4 + xl * 2 + xh
    else:
        x_first = xh * 8 + xl * 4 + yl * 2 + yh
        y_first = yh * 8 + yl * 4 + xl * 2 + xh
    keep = jnp.where(mc == 0, x_first, y_first)
    send = jnp.where(mc == 0, y_first, x_first)
    return [keep, send]


def attend_kernel(heads, *refs):
    place_ref, q_ref, do_ref, wk_ref, wv_ref, c4, c3, c2, c1, c0 = refs[:10]
    out_ref, gq_ref, send_ref, keep_ref, own_ref, p1_ref, p2_ref, p3_ref, p4_ref = refs[10:19]
    win, ct, absorbed, grad_lat, attended, grad_abs, grad_rope, acc = refs[19:]
    step = pl.program_id(0)
    scale = QDIM ** -0.5

    @pl.when(step == 0)
    def _():
        win[0:64] = c4[...]
        for n, c in enumerate((c3, c2, c1, c0)):
            win[64 + 128 * n : 192 + 128 * n] = c[...]
        for half in range(2):
            ct[half] = win[half * HALF : half * HALF + SEEN].T
        acc[...] = jnp.zeros_like(acc)

    for h in range(heads):
        q_n = q_ref[:, h * QDIM : h * QDIM + NOPE]
        q_r = q_ref[:, h * QDIM + NOPE : (h + 1) * QDIM]
        cols = slice(h * NOPE, (h + 1) * NOPE)
        a = dot(q_n, wk_ref[:, cols], 1, 1).astype(bf16)
        g = dot(do_ref[:, cols], wv_ref[:, cols], 1, 1).astype(bf16)
        for half in range(2):
            rows = slice(half * HALF, (half + 1) * HALF)
            to = slice(h * HALF, (h + 1) * HALF)
            absorbed[half, to, :LATENT] = a[rows]
            absorbed[half, to, LATENT:WIDE] = q_r[rows]
            grad_lat[half, to] = g[rows]

    own = c0[:, WIDE:PACKED].astype(f32)
    query_ids = own[:, 0:1] * 128.0 + own[:, 1:2]
    for half in range(2):
        rows = slice(half * HALF, (half + 1) * HALF)
        keys = slice(half * HALF, half * HALF + SEEN)
        id_rows = ct[half, WIDE : WIDE + 16].astype(f32)
        key_ids = id_rows[0:1] * 128.0 + id_rows[1:2]
        j = lax.broadcasted_iota(jnp.int32, (HALF, SEEN), 1)
        t = lax.broadcasted_iota(jnp.int32, (HALF, SEEN), 0)
        visible = (key_ids == query_ids[rows]) & (j - BACK <= t)
        bias = jnp.where(visible, 0.0, HIDDEN)

        a = absorbed[half][:, :WIDE]
        g = grad_lat[half]
        s = dot(a, ct[half][:WIDE]).reshape(heads, HALF, SEEN) * scale + bias[None]
        s = jnp.exp(s - jnp.max(s, axis=-1, keepdims=True))
        p = s * (1.0 / jnp.sum(s, axis=-1, keepdims=True))
        p_bf = p.astype(bf16).reshape(heads * HALF, SEEN)
        dp = dot(g, ct[half][:LATENT]).reshape(heads, HALF, SEEN)
        delta = jnp.sum(p * dp, axis=-1, keepdims=True)
        ds = (p * (dp - delta) * scale).astype(bf16).reshape(heads * HALF, SEEN)
        att = dot(p_bf, win[keys, :LATENT]).astype(bf16)
        ga = dot(ds, win[keys, :WIDE])
        ga_bf = ga[:, :LATENT].astype(bf16)
        for h in range(heads):
            of = slice(h * HALF, (h + 1) * HALF)
            attended[h, rows] = att[of]
            grad_abs[h, rows] = ga_bf[of]
            grad_rope[h, rows] = ga[of, LATENT:WIDE]
        acc[keys, :LATENT] += dot(p_bf, g, 0, 0)
        acc[keys] += dot(ds, a, 0, 0)

    core = place_ref[64]
    spots = [pl.multiple_of(place_ref[n] * CHUNK, CHUNK) for n in range(64)]
    for h in range(heads):
        cols = slice(h * NOPE, (h + 1) * NOPE)
        out_ref[:, cols] = dot(attended[h], wv_ref[:, cols]).astype(bf16)
        gq_ref[:, h * QDIM : h * QDIM + NOPE] = dot(grad_abs[h], wk_ref[:, cols])
        gq_ref[:, h * QDIM + NOPE : (h + 1) * QDIM] = grad_rope[h]
        dwk = dot(grad_abs[h], q_ref[:, h * QDIM : h * QDIM + NOPE], 0, 0).astype(bf16)
        dwv = dot(attended[h], do_ref[:, cols], 0, 0).astype(bf16)
        for m, dw in enumerate((dwk, dwv)):
            for n in range(16):
                zero = dw[2 * n * CHUNK : (2 * n + 1) * CHUNK]
                one = dw[(2 * n + 1) * CHUNK : (2 * n + 2) * CHUNK]
                keep, send = spots[32 * m + n], spots[32 * m + 16 + n]
                keep_ref[m, pl.ds(keep, CHUNK), cols] = jnp.where(core == 0, zero, one)
                send_ref[m, pl.ds(send, CHUNK), cols] = jnp.where(core == 0, one, zero)

    @pl.when(step == pl.num_programs(0) - 1)
    def _():
        p4_ref[...] = acc[0:64].astype(bf16)
        p3_ref[...] = acc[64:192].astype(bf16)
        p2_ref[...] = acc[192:320].astype(bf16)
        p1_ref[...] = acc[320:448].astype(bf16)
        own_ref[...] = acc[448:576]


def whole(shape):
    return pl.BlockSpec(shape, lambda i: (0,) * len(shape))


def part(rows, width):
    return pl.BlockSpec((rows, width), lambda i: (0, i))


def attend(steps, heads, places, blocks, queries, out_grad, w_uk, w_uv):
    all_heads = steps * heads
    rows = heads * HALF
    shapes = [
        jax.ShapeDtypeStruct((TOK, all_heads * NOPE), bf16),
        jax.ShapeDtypeStruct((TOK, all_heads * QDIM), f32),
        jax.ShapeDtypeStruct((2, LATENT // 2, all_heads * NOPE), bf16),
        jax.ShapeDtypeStruct((2, LATENT // 2, all_heads * NOPE), bf16),
        jax.ShapeDtypeStruct((TOK, WIDE), f32),
    ]
    shapes += [jax.ShapeDtypeStruct((TOK, WIDE), bf16)] * 3
    shapes += [jax.ShapeDtypeStruct((HALF, WIDE), bf16)]
    halves = pl.BlockSpec((2, LATENT // 2, heads * NOPE), lambda i: (0, 0, i))
    return pl.pallas_call(
        functools.partial(attend_kernel, heads),
        grid=(steps,),
        in_specs=[
            pl.BlockSpec(memory_space=pltpu.SMEM),
            part(TOK, heads * QDIM),
            part(TOK, heads * NOPE),
            part(LATENT, heads * NOPE),
            part(LATENT, heads * NOPE),
            whole((HALF, PACKED)),
        ]
        + [whole((TOK, PACKED))] * 4,
        out_specs=[part(TOK, heads * NOPE), part(TOK, heads * QDIM), halves, halves]
        + [whole(s.shape) for s in shapes[4:]],
        out_shape=shapes,
        scratch_shapes=[
            pltpu.VMEM((WINDOW, PACKED), bf16),
            pltpu.VMEM((2, PACKED, SEEN), bf16),
            pltpu.VMEM((2, rows, PACKED), bf16),
            pltpu.VMEM((2, rows, LATENT), bf16),
            pltpu.VMEM((heads, TOK, LATENT), bf16),
            pltpu.VMEM((heads, TOK, LATENT), bf16),
            pltpu.VMEM((heads, TOK, ROPE), f32),
            pltpu.VMEM((WINDOW, WIDE), f32),
        ],
        compiler_params=pltpu.CompilerParams(vmem_limit_bytes=54 * 2**20),
        cost_estimate=pl.CostEstimate(
            flops=int(18e9), bytes_accessed=16 * 2**20, transcendentals=2 * steps * rows * SEEN
        ),
    )(places, queries, out_grad, w_uk, w_uv, *blocks)


def passed_along(x, by):
    pairs = [(i, i + by) for i in range(N_CTX) if 0 <= i + by < N_CTX]
    return lax.ppermute(x, "ctx", pairs)


def over_core(send, keep):
    got = lax.ppermute(send, "ctx", [(i, i ^ 1) for i in range(N_CTX)])
    return (keep.astype(f32) + got.astype(f32)).astype(bf16)


def halved(x, pairs):
    h = x.shape[1] // 2
    got = lax.ppermute(x[:, :h], "ctx", pairs)
    return x[:, h:].astype(f32) + got.astype(f32)


def sum_over_head(x):
    me = lax.axis_index("head")
    odd = (me & 1) == 1
    low, high = x[:HALF], x[HALF:]
    swap = lambda y, d: lax.ppermute(y, "head", [(i, i ^ d) for i in range(8)])
    got = swap(jnp.where(odd, low, high).astype(bf16), 1)
    mine = jnp.where(odd, high, low) + got.astype(f32)
    for d in (2, 6):
        mine = mine.astype(bf16)
        mine = mine.astype(f32) + swap(mine, d).astype(f32)
    mine = mine.astype(bf16)
    other = swap(mine, 1)
    mine, other = mine.astype(f32), other.astype(f32)
    return jnp.concatenate([jnp.where(odd, other, mine), jnp.where(odd, mine, other)], axis=0)


def body(queries, latents, w_uk, w_uv, out_grad, doc_ids):
    ctx = lax.axis_index("ctx")
    number = doc_ids + 1
    packed = jnp.concatenate(
        [
            latents,
            (number // 128).astype(bf16)[:, None],
            (number % 128).astype(bf16)[:, None],
            jnp.zeros((TOK, PACKED - WIDE - 2), bf16),
        ],
        axis=1,
    )
    blocks = [passed_along(packed[HALF:], 4)]
    blocks += [passed_along(packed, d) for d in (3, 2, 1)] + [packed]
    places = chunk_places(ctx, 0) + chunk_places(ctx, 1) + [(ctx % 2)[None]]
    places = jnp.concatenate(places).astype(jnp.int32)
    res = attend(2, 8, places, blocks, queries, out_grad, w_uk, w_uv)
    outs, gq, send, keep, total, p1, p2, p3, p4 = res
    pieces = [passed_along(piece, -d) for d, piece in ((1, p1), (2, p2), (3, p3), (4, p4))]
    terms = over_core(send, keep)
    terms = [terms[:1], terms[1:]]
    stages = [halving_pairs(stream) for stream in range(2)]
    for n in range(2):
        terms = [halved(x, stages[g][n]).astype(bf16) for g, x in enumerate(terms)]
    for piece in pieces[:3]:
        total = total + piece.astype(f32)
    far = pieces[3].astype(f32)
    total = total + jnp.concatenate([jnp.zeros_like(far), far], axis=0)
    total = sum_over_head(total)
    x = jnp.concatenate(terms, axis=0)
    x = halved(x, stages[0][2]).astype(bf16)
    x = halved(x, stages[0][3])
    return outs, gq, total, x[0], x[1]


def solution(mesh):
    placed = (
        P("ctx", "head"),
        P("ctx", None),
        P(None, "head"),
        P(None, "head"),
        P("ctx", "head"),
        P("ctx"),
    )
    return jax.shard_map(
        body,
        mesh=mesh,
        in_specs=placed,
        out_specs=(
            P("ctx", "head"),
            P("ctx", "head"),
            P("ctx", None),
            P("ctx", "head"),
            P("ctx", "head"),
        ),
        check_vma=False,
    )
```

time: 119 us -> 104 us (0.87); the launches traced: 117 us -> 104 us
  starting transfers between devices: 50.2 us -> 41.9 us
  Pallas kernels: 20.8 us -> 17.8 us
  local copies, waits for them, and re-layouts: 6.87 us -> 5.15 us
  other arithmetic: 6.22 us -> 4.98 us
    ppermute x10 -> x7, starting transfers between devices: 19.9 us -> 12.6 us  [the longest x6 12.5 us: halved(): got = lax.ppermute(x[:, :h], 'ctx', pairs)]
    slice x12 -> x4, local copies, waits for them, and re-layouts: 3.3 us -> 0.15 us  [halved(): got = lax.ppermute(x[:, :h], 'ctx', pairs)]
    pallas_call x2 -> x1, Pallas kernels: 20.8 us -> 17.8 us  [attend(): pl.pallas_call(functools.partial(attend_kernel, heads), grid=(steps,), in...]
    ppermute x10 -> x7, waiting for transfers between devices: 12 us -> 14.9 us  [the longest x6 14.9 us: halved(): got = lax.ppermute(x[:, :h], 'ctx', pairs)]
    concatenate x3 -> x1, other arithmetic: 2.8 us -> 0.02 us  [body(): x = jnp.concatenate(terms, axis=0)]
    ppermute x4, waiting for transfers between devices: 8.91 us -> 6.53 us  [sum_over_head(): swap = lambda y, d: lax.ppermute(y, 'head', [(i, i ^ d) for i in range(8)])]
    convert_element_type x8 -> x5, other arithmetic: 2.41 us -> 2.94 us  [the longest x1 2.36 us: over_core(): return (keep.astype(f32) + got.astype(f32)).astype(bf16)]
  transfers between devices with their start and end apart: 22 -> 19, of which waited for: 12 -> 7; matrix products, arithmetic and copies ran while one was open for 8% -> 3% of each run, Pallas kernels for 0% -> 0%
where the time goes in v2:
time: 104 us
  starting transfers between devices  41.9 us (40%)
  waiting for transfers between devices  32.8 us (32%)
  Pallas kernels  17.8 us (17%)
  local copies, waits for them, and re-layouts  5.15 us (5%)
  other arithmetic  4.98 us (5%)
    ppermute x8, starting transfers between devices, passed_along(): return lax.ppermute(x, 'ctx', pairs)  19.4 us
    pallas_call x1, Pallas kernels, attend(): pl.pallas_call(functools.partial(attend_kernel, heads), grid=(steps,), in...  17.8 us
    ppermute x6, waiting for transfers between devices, halved(): got = lax.ppermute(x[:, :h], 'ctx', pairs)  14.9 us
    ppermute x6, starting transfers between devices, halved(): got = lax.ppermute(x[:, :h], 'ctx', pairs)  12.5 us
    ppermute x8, waiting for transfers between devices, passed_along(): return lax.ppermute(x, 'ctx', pairs)  11.3 us
    ppermute x4, starting transfers between devices, sum_over_head(): swap = lambda y, d: lax.ppermute(y, 'head', [(i, i ^ d) for i in range(8)])  9.87 us
    ppermute x4, waiting for transfers between devices, sum_over_head(): swap = lambda y, d: lax.ppermute(y, 'head', [(i, i ^ d) for i in range(8)])  6.53 us
    unnamed x12, local copies, waits for them, and re-layouts  3.31 us
  transfers between devices with their start and end apart: 19, of which 7 were waited for; matrix products, arithmetic and copies ran while one was open for 3% of the time, Pallas kernels for 0%

profile of v2, /device:TPU:32, one launch (start us, length us, event | category | flops | bytes accessed | tf_op | source)
XLA Modules:
  0.0 103.6 jit_solution(1211401378743340432)
XLA Ops:
  0.6 0.7 convert_bitcast_fusion
  1.3 0.1 copy.13
  1.4 0.1 copy.12
  1.6 1.1 %copy.11 = bf16[128,576]{1,0:T(8,128)(2,1)S(1)} copy(bf16[128,576]{0,1:T(8,128)(2,1)} %param.7) | data formatting | bytes 294912 | tf_op args[1]
  2.7 0.1 pad.9.clone
  2.7 0.1 maximum_maximum_fusion.refs_9_
  2.8 0.0 copy-start
  2.8 1.7 %collective-permute-start.3 = (bf16[128,640]{1,0:T(8,128)(2,1)S(1)}, bf16[128,640]{1,0:T(8,128)(2,1)S(1)}, u32[]{:S(2)}, u32[]{:S(2)}) collective-permute-start(bf16[128,640]{1,0:T(8,128)(2,1)S(1)} %maximum_maximum_fusion.refs_9_), channel_id=1, source_target_pairs={{0,8},{8,16},{16,24},{24,32},{32,40},{40,48},{48,56},{56,64},{64,7... | collective-permute-start | bytes 491528 | tf_op jit(solution)/shard_map/ppermute | solution.py:224
  4.6 3.6 %collective-permute-start.2 = (bf16[128,640]{1,0:T(8,128)(2,1)S(1)}, bf16[128,640]{1,0:T(8,128)(2,1)S(1)}, u32[]{:S(2)}, u32[]{:S(2)}) collective-permute-start(bf16[128,640]{1,0:T(8,128)(2,1)S(1)} %maximum_maximum_fusion.refs_9_), channel_id=1, source_target_pairs={{0,16},{8,24},{16,32},{24,40},{32,48},{40,56},{48,64},{56,72},{64,... | collective-permute-start | bytes 491528 | tf_op jit(solution)/shard_map/ppermute | solution.py:224
  8.2 4.0 %collective-permute-start.1 = (bf16[128,640]{1,0:T(8,128)(2,1)S(1)}, bf16[128,640]{1,0:T(8,128)(2,1)S(1)}, u32[]{:S(2)}, u32[]{:S(2)}) collective-permute-start(bf16[128,640]{1,0:T(8,128)(2,1)S(1)} %maximum_maximum_fusion.refs_9_), channel_id=1, source_target_pairs={{0,24},{8,32},{16,40},{24,48},{32,56},{40,64},{48,72},{56,80},{64,... | collective-permute-start | bytes 491528 | tf_op jit(solution)/shard_map/ppermute | solution.py:224
  12.2 4.9 %collective-permute-start = (bf16[64,640]{1,0:T(8,128)(2,1)S(1)}, bf16[64,640]{1,0:T(8,128)(2,1)S(1)}, u32[]{:S(2)}, u32[]{:S(2)}) collective-permute-start(bf16[64,640]{1,0:T(8,128)(2,1)S(1)} %slice.74), channel_id=1, source_target_pairs={{0,32},{8,40},{16,48},{24,56},{32,64},{40,72},{48,80},{56,88},{64,... | collective-permute-start | bytes 245768 | tf_op jit(solution)/shard_map/ppermute | solution.py:224
  17.2 0.6 concatenate.17.refs_0_
  17.9 1.3 %collective-permute-done.refs_5_ = bf16[64,640]{1,0:T(8,128)(2,1)S(1)} collective-permute-done((bf16[64,640]{1,0:T(8,128)(2,1)S(1)}, bf16[64,640]{1,0:T(8,128)(2,1)S(1)}, u32[]{:S(2)}, u32[]{:S(2)}) %collective-permute-start) | collective-permute-done | bytes 81952 | tf_op jit(solution)/shard_map/ppermute | solution.py:224
  19.2 0.0 copy-start.4
  19.2 0.0 collective-permute-done.3.refs_8_
  19.2 0.0 copy-start.1
  19.2 0.0 collective-permute-done.2.refs_7_
  19.2 0.0 copy-start.2
  19.2 0.0 collective-permute-done.1.refs_6_
  19.2 0.0 copy-done
  19.2 0.6 copy-done.4
  19.8 0.1 copy-done.1
  19.9 0.1 copy-done.2
  20.0 0.7 copy-done.3
  20.6 17.8 %shard_map.101 = (bf16[128,2048]{1,0:T(8,128)(2,1)}, f32[128,3072]{1,0:T(8,128)}, bf16[2,256,2048]{2,1,0:T(8,128)(2,1)}, bf16[2,256,2048]{2,1,0:T(8,128)(2,1)}, ...) custom-call(s32[65]{0:T(128)} %concatenate.17.refs_0_, ...), custom_call_target="tpu_custom_call" | custom-call | flops 17999998976 | bytes 16777216 | tf_op jit(solution)/shard_map/pallas_call | solution.py:190
  38.5 0.1 collective-permute-start.12
  38.6 1.3 %collective-permute-start.4 = (bf16[128,576]{1,0:T(8,128)(2,1)}, bf16[128,576]{1,0:T(8,128)(2,1)S(1)}, u32[]{:S(2)}, u32[]{:S(2)}) collective-permute-start(bf16[128,576]{1,0:T(8,128)(2,1)} %get-tuple-element.17), channel_id=1, source_target_pairs={{8,0},{16,8},{24,16},{32,24},{40,32},{48,40},{56,48},{64,56},{72,6... | collective-permute-start | bytes 442376 | tf_op jit(solution)/shard_map/ppermute | solution.py:224
  39.9 1.3 %collective-permute-start.5 = (bf16[128,576]{1,0:T(8,128)(2,1)}, bf16[128,576]{1,0:T(8,128)(2,1)S(1)}, u32[]{:S(2)}, u32[]{:S(2)}) collective-permute-start(bf16[128,576]{1,0:T(8,128)(2,1)} %get-tuple-element.18), channel_id=1, source_target_pairs={{16,0},{24,8},{32,16},{40,24},{48,32},{56,40},{64,48},{72,56},{80,... | collective-permute-start | bytes 442376 | tf_op jit(solution)/shard_map/ppermute | solution.py:224
  41.2 1.3 %collective-permute-start.6 = (bf16[128,576]{1,0:T(8,128)(2,1)}, bf16[128,576]{1,0:T(8,128)(2,1)S(1)}, u32[]{:S(2)}, u32[]{:S(2)}) collective-permute-start(bf16[128,576]{1,0:T(8,128)(2,1)} %get-tuple-element.19), channel_id=1, source_target_pairs={{24,0},{32,8},{40,16},{48,24},{56,32},{64,40},{72,48},{80,56},{88,... | collective-permute-start | bytes 442376 | tf_op jit(solution)/shard_map/ppermute | solution.py:224
  42.5 1.3 %collective-permute-start.7 = (bf16[64,576]{1,0:T(8,128)(2,1)}, bf16[64,576]{1,0:T(8,128)(2,1)S(1)}, u32[]{:S(2)}, u32[]{:S(2)}) collective-permute-start(bf16[64,576]{1,0:T(8,128)(2,1)} %get-tuple-element.20), channel_id=1, source_target_pairs={{32,0},{40,8},{48,16},{56,24},{64,32},{72,40},{80,48},{88,56},{96,... | collective-permute-start | bytes 221192 | tf_op jit(solution)/shard_map/ppermute | solution.py:224
  43.8 10.0 %collective-permute-done.7 = bf16[64,576]{1,0:T(8,128)(2,1)S(1)} collective-permute-done((bf16[64,576]{1,0:T(8,128)(2,1)}, bf16[64,576]{1,0:T(8,128)(2,1)S(1)}, u32[]{:S(2)}, u32[]{:S(2)}) %collective-permute-start.7) | collective-permute-done | bytes 73760 | tf_op jit(solution)/shard_map/ppermute | solution.py:224
  53.7 0.0 collective-permute-done.4
  53.7 0.0 collective-permute-done.5
  53.7 0.0 collective-permute-done.6
  53.7 1.1 %convert_add_fusion = f32[128,576]{1,0:T(8,128)S(1)} fusion(bf16[128,576]{1,0:T(8,128)(2,1)S(1)} %collective-permute-done.6, bf16[128,576]{1,0:T(8,128)(2,1)S(1)} %collective-permute-done.5, f32[128,576]{1,0:T(8,128)} %get-tuple-element.16, bf16[128,576]{1,0:T(8,128)(2,1)S(1)} %collective-permute-done.4, bf16[64,576]{1,0:T(8,128)(2,1)S(1)} %collective-permute-done.7), kind=kLoop, calls=%fused_computation.9 | loop fusion | flops 589824 | bytes 1105920 | tf_op jit(solution)/shard_map/add | solution.py:281
  54.8 0.0 collective-permute-done.12
  54.8 2.4 %add_convert_fusion = bf16[2,256,2048]{2,1,0:T(8,128)(2,1)S(1)} fusion(bf16[2,256,2048]{2,1,0:T(8,128)(2,1)S(1)} %collective-permute-done.12, bf16[2,256,2048]{2,1,0:T(8,128)(2,1)} %get-tuple-element.21), kind=kLoop, calls=%fused_computation | loop fusion | flops 4194304 | bytes 6291456 | tf_op jit(solution)/shard_map/convert_element_type | solution.py:229
  57.2 0.1 fusion.7
  57.3 4.5 %collective-permute-start.13 = (bf16[1,128,2048]{2,1,0:T(8,128)(2,1)S(1)}, bf16[1,128,2048]{2,1,0:T(8,128)(2,1)S(1)}, u32[]{:S(2)}, u32[]{:S(2)}) collective-permute-start(bf16[1,128,2048]{2,1,0:T(8,128)(2,1)S(1)} %get-tuple-element.32), channel_id=1, source_target_pairs={{0,16},{8,72},{16,0},{24,88},{32,48},{40,104},{48,32},{56,120},{64... | collective-permute-start | bytes 1572872 | tf_op jit(solution)/shard_map/ppermute | solution.py:234
  61.8 2.9 %collective-permute-start.15 = (bf16[1,128,2048]{2,1,0:T(8,128)(2,1)S(1)}, bf16[1,128,2048]{2,1,0:T(8,128)(2,1)S(1)}, u32[]{:S(2)}, u32[]{:S(2)}) collective-permute-start(bf16[1,128,2048]{2,1,0:T(8,128)(2,1)S(1)} %get-tuple-element.33), channel_id=1, source_target_pairs={{0,48},{8,200},{16,32},{24,216},{32,16},{40,232},{48,0},{56,248},{... | collective-permute-start | bytes 1572872 | tf_op jit(solution)/shard_map/ppermute | solution.py:234
  64.7 0.2 collective-permute-start.8
  64.9 4.8 %collective-permute-done.8 = bf16[64,576]{1,0:T(8,128)(2,1)S(1)} collective-permute-done((bf16[64,576]{1,0:T(8,128)(2,1)S(1)}, bf16[64,576]{1,0:T(8,128)(2,1)S(1)}, u32[]{:S(2)}, u32[]{:S(2)}) %collective-permute-start.8) | collective-permute-done | bytes 73760 | tf_op jit(solution)/shard_map/ppermute | solution.py:242
  69.7 3.5 %collective-permute-start.9 = (bf16[64,576]{1,0:T(8,128)(2,1)S(1)}, bf16[64,576]{1,0:T(8,128)(2,1)S(1)}, u32[]{:S(2)}, u32[]{:S(2)}) collective-permute-start(bf16[64,576]{1,0:T(8,128)(2,1)S(1)} %add_convert_fusion.8), channel_id=1, source_target_pairs={{0,2},{1,3},{2,0},{3,1},{4,6},{5,7},{6,4},{7,5},{8,10},{9,11},{10,... | collective-permute-start | bytes 221192 | tf_op jit(solution)/shard_map/ppermute | solution.py:242
  73.2 0.0 collective-permute-done.13
  73.2 0.0 collective-permute-done.15
  73.2 0.4 add_convert_fusion.2
  73.6 1.0 collective-permute-start.16
  74.6 1.8 %collective-permute-done.9 = bf16[64,576]{1,0:T(8,128)(2,1)S(1)} collective-permute-done((bf16[64,576]{1,0:T(8,128)(2,1)S(1)}, bf16[64,576]{1,0:T(8,128)(2,1)S(1)}, u32[]{:S(2)}, u32[]{:S(2)}) %collective-permute-start.9) | collective-permute-done | bytes 73760 | tf_op jit(solution)/shard_map/ppermute | solution.py:242
  76.4 5.8 %collective-permute-start.10 = (bf16[64,576]{1,0:T(8,128)(2,1)S(1)}, bf16[64,576]{1,0:T(8,128)(2,1)S(1)}, u32[]{:S(2)}, u32[]{:S(2)}) collective-permute-start(bf16[64,576]{1,0:T(8,128)(2,1)S(1)} %add_convert_fusion.7), channel_id=1, source_target_pairs={{0,6},{1,7},{2,4},{3,5},{4,2},{5,3},{6,0},{7,1},{8,14},{9,15},{10,... | collective-permute-start | bytes 221192 | tf_op jit(solution)/shard_map/ppermute | solution.py:242
  82.3 0.9 collective-permute-start.14
  83.2 0.0 collective-permute-done.16
  83.2 0.1 add_convert_fusion.4
  83.3 6.7 %collective-permute-done.14 = bf16[1,64,2048]{2,1,0:T(8,128)(2,1)S(1)} collective-permute-done((bf16[1,64,2048]{2,1,0:T(8,128)(2,1)S(1)}, bf16[1,64,2048]{2,1,0:T(8,128)(2,1)S(1)}, u32[]{:S(2)}, u32[]{:S(2)}) %collective-permute-start.14) | collective-permute-done | bytes 262176 | tf_op jit(solution)/shard_map/ppermute | solution.py:234
  89.9 0.1 add_convert_fusion.5
  90.0 1.5 %collective-permute-start.17 = (bf16[2,32,2048]{2,1,0:T(8,128)(2,1)S(1)}, bf16[2,32,2048]{2,1,0:T(8,128)(2,1)S(1)}, u32[]{:S(2)}, u32[]{:S(2)}) collective-permute-start(bf16[2,32,2048]{2,1,0:T(8,128)(2,1)S(1)} %pad_maximum_fusion.1), channel_id=1, source_target_pairs={{0,64},{8,24},{16,80},{24,8},{32,96},{40,56},{48,112},{56,40},{64,... | collective-permute-start | bytes 786440 | tf_op jit(solution)/shard_map/ppermute | solution.py:234
  91.5 0.0 collective-permute-done.10
  91.6 0.3 collective-permute-start.11
  91.9 4.6 %collective-permute-done.17 = bf16[2,32,2048]{2,1,0:T(8,128)(2,1)S(1)} collective-permute-done((bf16[2,32,2048]{2,1,0:T(8,128)(2,1)S(1)}, bf16[2,32,2048]{2,1,0:T(8,128)(2,1)S(1)}, u32[]{:S(2)}, u32[]{:S(2)}) %collective-permute-start.17) | collective-permute-done | bytes 262176 | tf_op jit(solution)/shard_map/ppermute | solution.py:234
  96.5 0.1 add_convert_fusion.3
  96.6 1.7 %collective-permute-start.18 = (bf16[2,16,2048]{2,1,0:T(8,128)(2,1)S(1)}, bf16[2,16,2048]{2,1,0:T(8,128)(2,1)S(1)}, u32[]{:S(2)}, u32[]{:S(2)}) collective-permute-start(bf16[2,16,2048]{2,1,0:T(8,128)(2,1)S(1)} %slice.88), channel_id=1, source_target_pairs={{0,192},{8,56},{16,208},{24,40},{32,224},{40,24},{48,240},{56,8},{... | collective-permute-start | bytes 393224 | tf_op jit(solution)/shard_map/ppermute | solution.py:234
  98.3 0.0 collective-permute-done.11
  98.3 0.9 copy.14
  99.2 3.6 %collective-permute-done.18 = bf16[2,16,2048]{2,1,0:T(8,128)(2,1)S(1)} collective-permute-done((bf16[2,16,2048]{2,1,0:T(8,128)(2,1)S(1)}, bf16[2,16,2048]{2,1,0:T(8,128)(2,1)S(1)}, u32[]{:S(2)}, u32[]{:S(2)}) %collective-permute-start.18) | collective-permute-done | bytes 131104 | tf_op jit(solution)/shard_map/ppermute | solution.py:234
  102.9 0.7 slice_bitcast_fusion
  (17 shorter events, 0.3 us)
Async XLA Ops:
  2.8 16.4 %copy-start = (bf16[128,640]{1,0:T(8,128)(2,1)}, bf16[128,640]{1,0:T(8,128)(2,1)S(1)}, u32[]{:S(2)}) copy-start(bf16[128,640]{1,0:T(8,128)(2,1)S(1)} %maximum_maximum_fusion.refs_9_) | copy-start | bytes 491524
  2.8 16.4 %collective-permute-start.3 = (bf16[128,640]{1,0:T(8,128)(2,1)S(1)}, bf16[128,640]{1,0:T(8,128)(2,1)S(1)}, u32[]{:S(2)}, u32[]{:S(2)}) collective-permute-start(bf16[128,640]{1,0:T(8,128)(2,1)S(1)} %maximum_maximum_fusion.refs_9_), channel_id=1, source_target_pairs={{0,8},{8,16},{16,24},{24,32},{32,40},{40,48},{48,56},{56,64},{64,7... | collective-permute-start | bytes 491528 | tf_op jit(solution)/shard_map/ppermute | solution.py:224
  4.6 14.6 %collective-permute-start.2 = (bf16[128,640]{1,0:T(8,128)(2,1)S(1)}, bf16[128,640]{1,0:T(8,128)(2,1)S(1)}, u32[]{:S(2)}, u32[]{:S(2)}) collective-permute-start(bf16[128,640]{1,0:T(8,128)(2,1)S(1)} %maximum_maximum_fusion.refs_9_), channel_id=1, source_target_pairs={{0,16},{8,24},{16,32},{24,40},{32,48},{40,56},{48,64},{56,72},{64,... | collective-permute-start | bytes 491528 | tf_op jit(solution)/shard_map/ppermute | solution.py:224
  8.2 11.0 %collective-permute-start.1 = (bf16[128,640]{1,0:T(8,128)(2,1)S(1)}, bf16[128,640]{1,0:T(8,128)(2,1)S(1)}, u32[]{:S(2)}, u32[]{:S(2)}) collective-permute-start(bf16[128,640]{1,0:T(8,128)(2,1)S(1)} %maximum_maximum_fusion.refs_9_), channel_id=1, source_target_pairs={{0,24},{8,32},{16,40},{24,48},{32,56},{40,64},{48,72},{56,80},{64,... | collective-permute-start | bytes 491528 | tf_op jit(solution)/shard_map/ppermute | solution.py:224
  12.2 7.0 %collective-permute-start = (bf16[64,640]{1,0:T(8,128)(2,1)S(1)}, bf16[64,640]{1,0:T(8,128)(2,1)S(1)}, u32[]{:S(2)}, u32[]{:S(2)}) collective-permute-start(bf16[64,640]{1,0:T(8,128)(2,1)S(1)} %slice.74), channel_id=1, source_target_pairs={{0,32},{8,40},{16,48},{24,56},{32,64},{40,72},{48,80},{56,88},{64,... | collective-permute-start | bytes 245768 | tf_op jit(solution)/shard_map/ppermute | solution.py:224
  19.2 0.6 copy-start.4
  19.2 0.7 copy-start.1
  19.2 0.7 copy-start.2
  20.0 0.7 copy-start.3
  38.5 16.4 %collective-permute-start.12 = (bf16[2,256,2048]{2,1,0:T(8,128)(2,1)}, bf16[2,256,2048]{2,1,0:T(8,128)(2,1)S(1)}, u32[]{:S(2)}, u32[]{:S(2)}) collective-permute-start(bf16[2,256,2048]{2,1,0:T(8,128)(2,1)} %get-tuple-element.22), channel_id=1, source_target_pairs={{0,8},{8,0},{16,24},{24,16},{32,40},{40,32},{48,56},{56,48},{64,72... | collective-permute-start | bytes 6291464 | tf_op jit(solution)/shard_map/ppermute | solution.py:228
  38.6 15.2 %collective-permute-start.4 = (bf16[128,576]{1,0:T(8,128)(2,1)}, bf16[128,576]{1,0:T(8,128)(2,1)S(1)}, u32[]{:S(2)}, u32[]{:S(2)}) collective-permute-start(bf16[128,576]{1,0:T(8,128)(2,1)} %get-tuple-element.17), channel_id=1, source_target_pairs={{8,0},{16,8},{24,16},{32,24},{40,32},{48,40},{56,48},{64,56},{72,6... | collective-permute-start | bytes 442376 | tf_op jit(solution)/shard_map/ppermute | solution.py:224
  39.9 13.9 %collective-permute-start.5 = (bf16[128,576]{1,0:T(8,128)(2,1)}, bf16[128,576]{1,0:T(8,128)(2,1)S(1)}, u32[]{:S(2)}, u32[]{:S(2)}) collective-permute-start(bf16[128,576]{1,0:T(8,128)(2,1)} %get-tuple-element.18), channel_id=1, source_target_pairs={{16,0},{24,8},{32,16},{40,24},{48,32},{56,40},{64,48},{72,56},{80,... | collective-permute-start | bytes 442376 | tf_op jit(solution)/shard_map/ppermute | solution.py:224
  41.2 12.6 %collective-permute-start.6 = (bf16[128,576]{1,0:T(8,128)(2,1)}, bf16[128,576]{1,0:T(8,128)(2,1)S(1)}, u32[]{:S(2)}, u32[]{:S(2)}) collective-permute-start(bf16[128,576]{1,0:T(8,128)(2,1)} %get-tuple-element.19), channel_id=1, source_target_pairs={{24,0},{32,8},{40,16},{48,24},{56,32},{64,40},{72,48},{80,56},{88,... | collective-permute-start | bytes 442376 | tf_op jit(solution)/shard_map/ppermute | solution.py:224
  42.5 11.3 %collective-permute-start.7 = (bf16[64,576]{1,0:T(8,128)(2,1)}, bf16[64,576]{1,0:T(8,128)(2,1)S(1)}, u32[]{:S(2)}, u32[]{:S(2)}) collective-permute-start(bf16[64,576]{1,0:T(8,128)(2,1)} %get-tuple-element.20), channel_id=1, source_target_pairs={{32,0},{40,8},{48,16},{56,24},{64,32},{72,40},{80,48},{88,56},{96,... | collective-permute-start | bytes 221192 | tf_op jit(solution)/shard_map/ppermute | solution.py:224
  57.3 15.9 %collective-permute-start.13 = (bf16[1,128,2048]{2,1,0:T(8,128)(2,1)S(1)}, bf16[1,128,2048]{2,1,0:T(8,128)(2,1)S(1)}, u32[]{:S(2)}, u32[]{:S(2)}) collective-permute-start(bf16[1,128,2048]{2,1,0:T(8,128)(2,1)S(1)} %get-tuple-element.32), channel_id=1, source_target_pairs={{0,16},{8,72},{16,0},{24,88},{32,48},{40,104},{48,32},{56,120},{64... | collective-permute-start | bytes 1572872 | tf_op jit(solution)/shard_map/ppermute | solution.py:234
  61.8 11.4 %collective-permute-start.15 = (bf16[1,128,2048]{2,1,0:T(8,128)(2,1)S(1)}, bf16[1,128,2048]{2,1,0:T(8,128)(2,1)S(1)}, u32[]{:S(2)}, u32[]{:S(2)}) collective-permute-start(bf16[1,128,2048]{2,1,0:T(8,128)(2,1)S(1)} %get-tuple-element.33), channel_id=1, source_target_pairs={{0,48},{8,200},{16,32},{24,216},{32,16},{40,232},{48,0},{56,248},{... | collective-permute-start | bytes 1572872 | tf_op jit(solution)/shard_map/ppermute | solution.py:234
  64.7 5.0 %collective-permute-start.8 = (bf16[64,576]{1,0:T(8,128)(2,1)S(1)}, bf16[64,576]{1,0:T(8,128)(2,1)S(1)}, u32[]{:S(2)}, u32[]{:S(2)}) collective-permute-start(bf16[64,576]{1,0:T(8,128)(2,1)S(1)} %select_convert_fusion), channel_id=1, source_target_pairs={{0,1},{1,0},{2,3},{3,2},{4,5},{5,4},{6,7},{7,6},{8,9},{9,8},{10,11... | collective-permute-start | bytes 221192 | tf_op jit(solution)/shard_map/ppermute | solution.py:242
  69.7 6.7 %collective-permute-start.9 = (bf16[64,576]{1,0:T(8,128)(2,1)S(1)}, bf16[64,576]{1,0:T(8,128)(2,1)S(1)}, u32[]{:S(2)}, u32[]{:S(2)}) collective-permute-start(bf16[64,576]{1,0:T(8,128)(2,1)S(1)} %add_convert_fusion.8), channel_id=1, source_target_pairs={{0,2},{1,3},{2,0},{3,1},{4,6},{5,7},{6,4},{7,5},{8,10},{9,11},{10,... | collective-permute-start | bytes 221192 | tf_op jit(solution)/shard_map/ppermute | solution.py:242
  73.6 9.6 %collective-permute-start.16 = (bf16[1,64,2048]{2,1,0:T(8,128)(2,1)S(1)}, bf16[1,64,2048]{2,1,0:T(8,128)(2,1)S(1)}, u32[]{:S(2)}, u32[]{:S(2)}) collective-permute-start(bf16[1,64,2048]{2,1,0:T(8,128)(2,1)S(1)} %slice.84), channel_id=1, source_target_pairs={{0,16},{8,72},{16,0},{24,88},{32,48},{40,104},{48,32},{56,120},{64... | collective-permute-start | bytes 786440 | tf_op jit(solution)/shard_map/ppermute | solution.py:234
  76.4 15.1 %collective-permute-start.10 = (bf16[64,576]{1,0:T(8,128)(2,1)S(1)}, bf16[64,576]{1,0:T(8,128)(2,1)S(1)}, u32[]{:S(2)}, u32[]{:S(2)}) collective-permute-start(bf16[64,576]{1,0:T(8,128)(2,1)S(1)} %add_convert_fusion.7), channel_id=1, source_target_pairs={{0,6},{1,7},{2,4},{3,5},{4,2},{5,3},{6,0},{7,1},{8,14},{9,15},{10,... | collective-permute-start | bytes 221192 | tf_op jit(solution)/shard_map/ppermute | solution.py:242
  82.3 7.7 %collective-permute-start.14 = (bf16[1,64,2048]{2,1,0:T(8,128)(2,1)S(1)}, bf16[1,64,2048]{2,1,0:T(8,128)(2,1)S(1)}, u32[]{:S(2)}, u32[]{:S(2)}) collective-permute-start(bf16[1,64,2048]{2,1,0:T(8,128)(2,1)S(1)} %slice.80), channel_id=1, source_target_pairs={{0,48},{8,200},{16,32},{24,216},{32,16},{40,232},{48,0},{56,248},{... | collective-permute-start | bytes 786440 | tf_op jit(solution)/shard_map/ppermute | solution.py:234
  90.0 6.5 %collective-permute-start.17 = (bf16[2,32,2048]{2,1,0:T(8,128)(2,1)S(1)}, bf16[2,32,2048]{2,1,0:T(8,128)(2,1)S(1)}, u32[]{:S(2)}, u32[]{:S(2)}) collective-permute-start(bf16[2,32,2048]{2,1,0:T(8,128)(2,1)S(1)} %pad_maximum_fusion.1), channel_id=1, source_target_pairs={{0,64},{8,24},{16,80},{24,8},{32,96},{40,56},{48,112},{56,40},{64,... | collective-permute-start | bytes 786440 | tf_op jit(solution)/shard_map/ppermute | solution.py:234
  91.6 6.7 %collective-permute-start.11 = (bf16[64,576]{1,0:T(8,128)(2,1)S(1)}, bf16[64,576]{1,0:T(8,128)(2,1)S(1)}, u32[]{:S(2)}, u32[]{:S(2)}) collective-permute-start(bf16[64,576]{1,0:T(8,128)(2,1)S(1)} %add_convert_fusion.6), channel_id=1, source_target_pairs={{0,1},{1,0},{2,3},{3,2},{4,5},{5,4},{6,7},{7,6},{8,9},{9,8},{10,11... | collective-permute-start | bytes 221192 | tf_op jit(solution)/shard_map/ppermute | solution.py:242
  96.6 6.3 %collective-permute-start.18 = (bf16[2,16,2048]{2,1,0:T(8,128)(2,1)S(1)}, bf16[2,16,2048]{2,1,0:T(8,128)(2,1)S(1)}, u32[]{:S(2)}, u32[]{:S(2)}) collective-permute-start(bf16[2,16,2048]{2,1,0:T(8,128)(2,1)S(1)} %slice.88), channel_id=1, source_target_pairs={{0,192},{8,56},{16,208},{24,40},{32,224},{40,24},{48,240},{56,8},{... | collective-permute-start | bytes 393224 | tf_op jit(solution)/shard_map/ppermute | solution.py:234

commit v3 on v2

--- a/solution.py
+++ b/solution.py
@@ -43,23 +43,18 @@
 FAR = {0: 3, 3: 0, 1: 2, 2: 1}
 
 
-def halving_pairs(stream):
-    order = (NEAR, FAR) if stream == 0 else (FAR, NEAR)
-    stages = []
-    for turn, steps in ((0, order), (1, (NEAR, FAR))):
-        for step in steps:
-            pairs = []
-            for i in range(N_CTX):
-                y, x, c = place(i)
-                if c == turn:
-                    pairs.append((i, index_of(y, step[x], c)))
-                else:
-                    pairs.append((i, index_of(step[y], x, c)))
-            stages.append(pairs)
-    return stages
-
-
-def chunk_places(me, stream):
+OPPOSITE = {0: 2, 2: 0, 1: 3, 3: 1}
+
+
+def ring_pairs(turn, step):
+    pairs = []
+    for i in range(N_CTX):
+        y, x, c = place(i)
+        pairs.append((i, index_of(y, step[x], c) if c == turn else index_of(step[y], x, c)))
+    return pairs
+
+
+def chunk_places(me):
     chips = jnp.arange(16, dtype=jnp.int32)
     my, mx, mc = me // 8, (me // 2) % 4, me % 2
 
@@ -68,12 +63,8 @@
         return same & 1, same >> 1
 
     (xl, xh), (yl, yh) = bits(mx, chips % 4), bits(my, chips // 4)
-    if stream == 0:
-        x_first = xl * 8 + xh * 4 + yl * 2 + yh
-        y_first = yl * 8 + yh * 4 + xl * 2 + xh
-    else:
-        x_first = xh * 8 + xl * 4 + yl * 2 + yh
-        y_first = yh * 8 + yl * 4 + xl * 2 + xh
+    x_first = xl * 8 + xh * 4 + yl * 2 + yh
+    y_first = yl * 8 + yh * 4 + xl * 2 + xh
     keep = jnp.where(mc == 0, x_first, y_first)
     send = jnp.where(mc == 0, y_first, x_first)
     return [keep, send]
@@ -229,10 +220,13 @@
     return (keep.astype(f32) + got.astype(f32)).astype(bf16)
 
 
-def halved(x, pairs):
-    h = x.shape[1] // 2
-    got = lax.ppermute(x[:, :h], "ctx", pairs)
-    return x[:, h:].astype(f32) + got.astype(f32)
+def over_ring(x, turn):
+    q = x.shape[1] // 4
+    gots = [
+        lax.ppermute(x[:, n * q : (n + 1) * q], "ctx", ring_pairs(turn, step))
+        for n, step in enumerate((OPPOSITE, NEAR, FAR))
+    ]
+    return x[:, 3 * q :], gots
 
 
 def sum_over_head(x):
@@ -265,25 +259,22 @@
     )
     blocks = [passed_along(packed[HALF:], 4)]
     blocks += [passed_along(packed, d) for d in (3, 2, 1)] + [packed]
-    places = chunk_places(ctx, 0) + chunk_places(ctx, 1) + [(ctx % 2)[None]]
+    places = chunk_places(ctx) + chunk_places(ctx) + [(ctx % 2)[None]]
     places = jnp.concatenate(places).astype(jnp.int32)
     res = attend(2, 8, places, blocks, queries, out_grad, w_uk, w_uv)
     outs, gq, send, keep, total, p1, p2, p3, p4 = res
     pieces = [passed_along(piece, -d) for d, piece in ((1, p1), (2, p2), (3, p3), (4, p4))]
     terms = over_core(send, keep)
-    terms = [terms[:1], terms[1:]]
-    stages = [halving_pairs(stream) for stream in range(2)]
-    for n in range(2):
-        terms = [halved(x, stages[g][n]).astype(bf16) for g, x in enumerate(terms)]
+    keep, gots = over_ring(terms, 0)
+    terms = sum((g.astype(f32) for g in gots), keep.astype(f32)).astype(bf16)
     for piece in pieces[:3]:
         total = total + piece.astype(f32)
     far = pieces[3].astype(f32)
     total = total + jnp.concatenate([jnp.zeros_like(far), far], axis=0)
     total = sum_over_head(total)
-    x = jnp.concatenate(terms, axis=0)
-    x = halved(x, stages[0][2]).astype(bf16)
-    x = halved(x, stages[0][3])
-    return outs, gq, total, x[0], x[1]
+    keep, gots = over_ring(terms, 1)
+    w_uk_grad, w_uv_grad = (sum((g[m].astype(f32) for g in gots), keep[m].astype(f32)) for m in range(2))
+    return outs, gq, total, w_uk_grad, w_uv_grad
 
 
 def solution(mesh):

time: 104 us -> 97.4 us (0.937)
  waiting for transfers between devices: 32.8 us -> 28.8 us
  starting transfers between devices: 41.9 us -> 39.3 us
    ppermute x6, waiting for transfers between devices: 14.9 us -> 9.4 us  [over_ring(): lax.ppermute(x[:, n * q:(n + 1) * q], 'ctx', ring_pairs(turn, step))]
    ppermute x4, starting transfers between devices: 9.87 us -> 7.3 us  [sum_over_head(): swap = lambda y, d: lax.ppermute(y, 'head', [(i, i ^ d) for i in range(8)])]
    ppermute x4, waiting for transfers between devices: 6.53 us -> 8.08 us  [sum_over_head(): swap = lambda y, d: lax.ppermute(y, 'head', [(i, i ^ d) for i in range(8)])]
  transfers between devices with their start and end apart: 19 -> 19, of which waited for: 7 -> 8; matrix products, arithmetic and copies ran while one was open for 3% -> 6% of each run, Pallas kernels for 0% -> 0%
where the time goes in v3:
time: 97.4 us; the launch traced here: 96.8 us
  starting transfers between devices  39.3 us (40%)
  waiting for transfers between devices  28.8 us (30%)
  Pallas kernels  17.8 us (18%)
  other arithmetic  5.44 us (6%)
  local copies, waits for them, and re-layouts  4.44 us (5%)
    ppermute x8, starting transfers between devices, passed_along(): return lax.ppermute(x, 'ctx', pairs)  19.4 us
    pallas_call x1, Pallas kernels, attend(): pl.pallas_call(functools.partial(attend_kernel, heads), grid=(steps,), in...  17.8 us
    ppermute x6, starting transfers between devices, over_ring(): lax.ppermute(x[:, n * q:(n + 1) * q], 'ctx', ring_pairs(turn, step))  12.5 us
    ppermute x8, waiting for transfers between devices, passed_along(): return lax.ppermute(x, 'ctx', pairs)  11.3 us
    ppermute x6, waiting for transfers between devices, over_ring(): lax.ppermute(x[:, n * q:(n + 1) * q], 'ctx', ring_pairs(turn, step))  9.4 us
    ppermute x4, waiting for transfers between devices, sum_over_head(): swap = lambda y, d: lax.ppermute(y, 'head', [(i, i ^ d) for i in range(8)])  8.08 us
    ppermute x4, starting transfers between devices, sum_over_head(): swap = lambda y, d: lax.ppermute(y, 'head', [(i, i ^ d) for i in range(8)])  7.3 us
    unnamed x12, local copies, waits for them, and re-layouts  3.31 us
  transfers between devices with their start and end apart: 19, of which 8 were waited for; matrix products, arithmetic and copies ran while one was open for 6% of the time, Pallas kernels for 0%

profile of v3, /device:TPU:32, one launch (start us, length us, event | category | flops | bytes accessed | tf_op | source)
XLA Modules:
  0.0 96.8 jit_solution(11714981120748494835)
XLA Ops:
  0.6 0.7 convert_bitcast_fusion
  1.3 0.1 copy.13
  1.4 0.1 copy.12
  1.6 1.1 %copy.11 = bf16[128,576]{1,0:T(8,128)(2,1)S(1)} copy(bf16[128,576]{0,1:T(8,128)(2,1)} %param.7) | data formatting | bytes 294912 | tf_op args[1]
  2.7 0.1 pad.7.clone
  2.7 0.1 maximum_maximum_fusion.refs_9_
  2.8 0.0 copy-start
  2.8 1.7 %collective-permute-start.3 = (bf16[128,640]{1,0:T(8,128)(2,1)S(1)}, bf16[128,640]{1,0:T(8,128)(2,1)S(1)}, u32[]{:S(2)}, u32[]{:S(2)}) collective-permute-start(bf16[128,640]{1,0:T(8,128)(2,1)S(1)} %maximum_maximum_fusion.refs_9_), channel_id=1, source_target_pairs={{0,8},{8,16},{16,24},{24,32},{32,40},{40,48},{48,56},{56,64},{64,7... | collective-permute-start | bytes 491528 | tf_op jit(solution)/shard_map/ppermute | solution.py:215
  4.6 3.6 %collective-permute-start.2 = (bf16[128,640]{1,0:T(8,128)(2,1)S(1)}, bf16[128,640]{1,0:T(8,128)(2,1)S(1)}, u32[]{:S(2)}, u32[]{:S(2)}) collective-permute-start(bf16[128,640]{1,0:T(8,128)(2,1)S(1)} %maximum_maximum_fusion.refs_9_), channel_id=1, source_target_pairs={{0,16},{8,24},{16,32},{24,40},{32,48},{40,56},{48,64},{56,72},{64,... | collective-permute-start | bytes 491528 | tf_op jit(solution)/shard_map/ppermute | solution.py:215
  8.2 4.0 %collective-permute-start.1 = (bf16[128,640]{1,0:T(8,128)(2,1)S(1)}, bf16[128,640]{1,0:T(8,128)(2,1)S(1)}, u32[]{:S(2)}, u32[]{:S(2)}) collective-permute-start(bf16[128,640]{1,0:T(8,128)(2,1)S(1)} %maximum_maximum_fusion.refs_9_), channel_id=1, source_target_pairs={{0,24},{8,32},{16,40},{24,48},{32,56},{40,64},{48,72},{56,80},{64,... | collective-permute-start | bytes 491528 | tf_op jit(solution)/shard_map/ppermute | solution.py:215
  12.2 4.9 %collective-permute-start = (bf16[64,640]{1,0:T(8,128)(2,1)S(1)}, bf16[64,640]{1,0:T(8,128)(2,1)S(1)}, u32[]{:S(2)}, u32[]{:S(2)}) collective-permute-start(bf16[64,640]{1,0:T(8,128)(2,1)S(1)} %slice.75), channel_id=1, source_target_pairs={{0,32},{8,40},{16,48},{24,56},{32,64},{40,72},{48,80},{56,88},{64,... | collective-permute-start | bytes 245768 | tf_op jit(solution)/shard_map/ppermute | solution.py:215
  17.2 0.6 concatenate.14.refs_0_
  17.9 1.3 %collective-permute-done.refs_5_ = bf16[64,640]{1,0:T(8,128)(2,1)S(1)} collective-permute-done((bf16[64,640]{1,0:T(8,128)(2,1)S(1)}, bf16[64,640]{1,0:T(8,128)(2,1)S(1)}, u32[]{:S(2)}, u32[]{:S(2)}) %collective-permute-start) | collective-permute-done | bytes 81952 | tf_op jit(solution)/shard_map/ppermute | solution.py:215
  19.2 0.0 copy-start.4
  19.2 0.0 collective-permute-done.3.refs_8_
  19.2 0.0 copy-start.1
  19.2 0.0 collective-permute-done.2.refs_7_
  19.2 0.0 copy-start.2
  19.2 0.0 collective-permute-done.1.refs_6_
  19.2 0.0 copy-done
  19.2 0.6 copy-done.4
  19.8 0.1 copy-done.1
  19.9 0.0 copy-done.2
  20.0 0.0 copy-start.3
  20.0 0.7 copy-done.3
  20.6 17.8 %shard_map.101 = (bf16[128,2048]{1,0:T(8,128)(2,1)}, f32[128,3072]{1,0:T(8,128)}, bf16[2,256,2048]{2,1,0:T(8,128)(2,1)}, bf16[2,256,2048]{2,1,0:T(8,128)(2,1)}, ...) custom-call(s32[65]{0:T(128)} %concatenate.14.refs_0_, ...), custom_call_target="tpu_custom_call" | custom-call | flops 17999998976 | bytes 16777216 | tf_op jit(solution)/shard_map/pallas_call | solution.py:181
  38.5 0.1 collective-permute-start.12
  38.6 1.3 %collective-permute-start.4 = (bf16[128,576]{1,0:T(8,128)(2,1)}, bf16[128,576]{1,0:T(8,128)(2,1)S(1)}, u32[]{:S(2)}, u32[]{:S(2)}) collective-permute-start(bf16[128,576]{1,0:T(8,128)(2,1)} %get-tuple-element.17), channel_id=1, source_target_pairs={{8,0},{16,8},{24,16},{32,24},{40,32},{48,40},{56,48},{64,56},{72,6... | collective-permute-start | bytes 442376 | tf_op jit(solution)/shard_map/ppermute | solution.py:215
  39.9 1.3 %collective-permute-start.5 = (bf16[128,576]{1,0:T(8,128)(2,1)}, bf16[128,576]{1,0:T(8,128)(2,1)S(1)}, u32[]{:S(2)}, u32[]{:S(2)}) collective-permute-start(bf16[128,576]{1,0:T(8,128)(2,1)} %get-tuple-element.18), channel_id=1, source_target_pairs={{16,0},{24,8},{32,16},{40,24},{48,32},{56,40},{64,48},{72,56},{80,... | collective-permute-start | bytes 442376 | tf_op jit(solution)/shard_map/ppermute | solution.py:215
  41.2 1.3 %collective-permute-start.6 = (bf16[128,576]{1,0:T(8,128)(2,1)}, bf16[128,576]{1,0:T(8,128)(2,1)S(1)}, u32[]{:S(2)}, u32[]{:S(2)}) collective-permute-start(bf16[128,576]{1,0:T(8,128)(2,1)} %get-tuple-element.19), channel_id=1, source_target_pairs={{24,0},{32,8},{40,16},{48,24},{56,32},{64,40},{72,48},{80,56},{88,... | collective-permute-start | bytes 442376 | tf_op jit(solution)/shard_map/ppermute | solution.py:215
  42.5 1.3 %collective-permute-start.7 = (bf16[64,576]{1,0:T(8,128)(2,1)}, bf16[64,576]{1,0:T(8,128)(2,1)S(1)}, u32[]{:S(2)}, u32[]{:S(2)}) collective-permute-start(bf16[64,576]{1,0:T(8,128)(2,1)} %get-tuple-element.20), channel_id=1, source_target_pairs={{32,0},{40,8},{48,16},{56,24},{64,32},{72,40},{80,48},{88,56},{96,... | collective-permute-start | bytes 221192 | tf_op jit(solution)/shard_map/ppermute | solution.py:215
  43.8 10.0 %collective-permute-done.7 = bf16[64,576]{1,0:T(8,128)(2,1)S(1)} collective-permute-done((bf16[64,576]{1,0:T(8,128)(2,1)}, bf16[64,576]{1,0:T(8,128)(2,1)S(1)}, u32[]{:S(2)}, u32[]{:S(2)}) %collective-permute-start.7) | collective-permute-done | bytes 73760 | tf_op jit(solution)/shard_map/ppermute | solution.py:215
  53.7 0.0 collective-permute-done.4
  53.7 0.0 collective-permute-done.5
  53.7 0.0 collective-permute-done.6
  53.7 1.1 %convert_add_fusion = f32[128,576]{1,0:T(8,128)S(1)} fusion(bf16[128,576]{1,0:T(8,128)(2,1)S(1)} %collective-permute-done.6, bf16[128,576]{1,0:T(8,128)(2,1)S(1)} %collective-permute-done.5, f32[128,576]{1,0:T(8,128)} %get-tuple-element.16, bf16[128,576]{1,0:T(8,128)(2,1)S(1)} %collective-permute-done.4, bf16[64,576]{1,0:T(8,128)(2,1)S(1)} %collective-permute-done.7), kind=kLoop, calls=%fused_computation.3 | loop fusion | flops 589824 | bytes 1105920 | tf_op jit(solution)/shard_map/add | solution.py:273
  54.8 0.2 collective-permute-start.8
  55.0 4.3 %collective-permute-done.8 = bf16[64,576]{1,0:T(8,128)(2,1)S(1)} collective-permute-done((bf16[64,576]{1,0:T(8,128)(2,1)S(1)}, bf16[64,576]{1,0:T(8,128)(2,1)S(1)}, u32[]{:S(2)}, u32[]{:S(2)}) %collective-permute-start.8) | collective-permute-done | bytes 73760 | tf_op jit(solution)/shard_map/ppermute | solution.py:236
  59.4 3.4 %collective-permute-start.9 = (bf16[64,576]{1,0:T(8,128)(2,1)S(1)}, bf16[64,576]{1,0:T(8,128)(2,1)S(1)}, u32[]{:S(2)}, u32[]{:S(2)}) collective-permute-start(bf16[64,576]{1,0:T(8,128)(2,1)S(1)} %add_convert_fusion.4), channel_id=1, source_target_pairs={{0,2},{1,3},{2,0},{3,1},{4,6},{5,7},{6,4},{7,5},{8,10},{9,11},{10,... | collective-permute-start | bytes 221192 | tf_op jit(solution)/shard_map/ppermute | solution.py:236
  62.7 0.0 collective-permute-done.12
  62.7 2.4 %add_convert_fusion = bf16[2,256,2048]{2,1,0:T(8,128)(2,1)S(1)} fusion(bf16[2,256,2048]{2,1,0:T(8,128)(2,1)S(1)} %collective-permute-done.12, bf16[2,256,2048]{2,1,0:T(8,128)(2,1)} %get-tuple-element.21), kind=kLoop, calls=%fused_computation | loop fusion | flops 4194304 | bytes 6291456 | tf_op jit(solution)/shard_map/convert_element_type | solution.py:220
  65.1 0.1 fusion.6
  65.2 4.9 %collective-permute-start.13 = (bf16[2,64,2048]{2,1,0:T(8,128)(2,1)S(1)}, bf16[2,64,2048]{2,1,0:T(8,128)(2,1)S(1)}, u32[]{:S(2)}, u32[]{:S(2)}) collective-permute-start(bf16[2,64,2048]{2,1,0:T(8,128)(2,1)S(1)} %get-tuple-element.30), channel_id=1, source_target_pairs={{0,32},{8,136},{16,48},{24,152},{32,0},{40,168},{48,16},{56,184},{... | collective-permute-start | bytes 1572872 | tf_op jit(solution)/shard_map/ppermute | solution.py:226
  70.1 2.5 %collective-permute-start.15 = (bf16[2,64,2048]{2,1,0:T(8,128)(2,1)S(1)}, bf16[2,64,2048]{2,1,0:T(8,128)(2,1)S(1)}, u32[]{:S(2)}, u32[]{:S(2)}) collective-permute-start(bf16[2,64,2048]{2,1,0:T(8,128)(2,1)S(1)} %get-tuple-element.31), channel_id=1, source_target_pairs={{0,48},{8,200},{16,32},{24,216},{32,16},{40,232},{48,0},{56,248},{... | collective-permute-start | bytes 1572872 | tf_op jit(solution)/shard_map/ppermute | solution.py:226
  72.6 0.8 collective-permute-start.14
  73.4 0.0 collective-permute-done.9
  73.4 3.7 %collective-permute-start.10 = (bf16[64,576]{1,0:T(8,128)(2,1)S(1)}, bf16[64,576]{1,0:T(8,128)(2,1)S(1)}, u32[]{:S(2)}, u32[]{:S(2)}) collective-permute-start(bf16[64,576]{1,0:T(8,128)(2,1)S(1)} %add_convert_fusion.3), channel_id=1, source_target_pairs={{0,6},{1,7},{2,4},{3,5},{4,2},{5,3},{6,0},{7,1},{8,14},{9,15},{10,... | collective-permute-start | bytes 221192 | tf_op jit(solution)/shard_map/ppermute | solution.py:236
  77.1 3.7 %collective-permute-done.10 = bf16[64,576]{1,0:T(8,128)(2,1)S(1)} collective-permute-done((bf16[64,576]{1,0:T(8,128)(2,1)S(1)}, bf16[64,576]{1,0:T(8,128)(2,1)S(1)}, u32[]{:S(2)}, u32[]{:S(2)}) %collective-permute-start.10) | collective-permute-done | bytes 73760 | tf_op jit(solution)/shard_map/ppermute | solution.py:236
  80.8 0.1 collective-permute-start.11
  80.9 0.0 collective-permute-done.13
  81.0 4.0 %collective-permute-done.15 = bf16[2,64,2048]{2,1,0:T(8,128)(2,1)S(1)} collective-permute-done((bf16[2,64,2048]{2,1,0:T(8,128)(2,1)S(1)}, bf16[2,64,2048]{2,1,0:T(8,128)(2,1)S(1)}, u32[]{:S(2)}, u32[]{:S(2)}) %collective-permute-start.15) | collective-permute-done | bytes 524320 | tf_op jit(solution)/shard_map/ppermute | solution.py:226
  84.9 1.3 %collective-permute-done.14 = bf16[2,64,2048]{2,1,0:T(8,128)(2,1)S(1)} collective-permute-done((bf16[2,64,2048]{2,1,0:T(8,128)(2,1)S(1)}, bf16[2,64,2048]{2,1,0:T(8,128)(2,1)S(1)}, u32[]{:S(2)}, u32[]{:S(2)}) %collective-permute-start.14) | collective-permute-done | bytes 524320 | tf_op jit(solution)/shard_map/ppermute | solution.py:226
  86.2 0.3 add_convert_fusion.1
  86.6 3.2 %collective-permute-start.16 = (bf16[2,16,2048]{2,1,0:T(8,128)(2,1)S(1)}, bf16[2,16,2048]{2,1,0:T(8,128)(2,1)S(1)}, u32[]{:S(2)}, u32[]{:S(2)}) collective-permute-start(bf16[2,16,2048]{2,1,0:T(8,128)(2,1)S(1)} %get-tuple-element.35), channel_id=1, source_target_pairs={{0,128},{8,40},{16,144},{24,56},{32,160},{40,8},{48,176},{56,24},{... | collective-permute-start | bytes 393224 | tf_op jit(solution)/shard_map/ppermute | solution.py:226
  89.8 1.1 %collective-permute-start.18 = (bf16[2,16,2048]{2,1,0:T(8,128)(2,1)S(1)}, bf16[2,16,2048]{2,1,0:T(8,128)(2,1)S(1)}, u32[]{:S(2)}, u32[]{:S(2)}) collective-permute-start(bf16[2,16,2048]{2,1,0:T(8,128)(2,1)S(1)} %get-tuple-element.36), channel_id=1, source_target_pairs={{0,192},{8,56},{16,208},{24,40},{32,224},{40,24},{48,240},{56,8},{... | collective-permute-start | bytes 393224 | tf_op jit(solution)/shard_map/ppermute | solution.py:226
  90.9 0.0 collective-permute-start.17
  90.9 0.0 collective-permute-done.11
  91.0 0.9 copy.14
  91.8 1.3 %collective-permute-done.16 = bf16[2,16,2048]{2,1,0:T(8,128)(2,1)S(1)} collective-permute-done((bf16[2,16,2048]{2,1,0:T(8,128)(2,1)S(1)}, bf16[2,16,2048]{2,1,0:T(8,128)(2,1)S(1)}, u32[]{:S(2)}, u32[]{:S(2)}) %collective-permute-start.16) | collective-permute-done | bytes 131104 | tf_op jit(solution)/shard_map/ppermute | solution.py:226
  93.1 2.9 %collective-permute-done.18 = bf16[2,16,2048]{2,1,0:T(8,128)(2,1)S(1)} collective-permute-done((bf16[2,16,2048]{2,1,0:T(8,128)(2,1)S(1)}, bf16[2,16,2048]{2,1,0:T(8,128)(2,1)S(1)}, u32[]{:S(2)}, u32[]{:S(2)}) %collective-permute-start.18) | collective-permute-done | bytes 131104 | tf_op jit(solution)/shard_map/ppermute | solution.py:226
  96.0 0.0 collective-permute-done.17
  96.0 0.8 add_bitcast_fusion
  (11 shorter events, 0.2 us)
Async XLA Ops:
  2.8 16.4 %copy-start = (bf16[128,640]{1,0:T(8,128)(2,1)}, bf16[128,640]{1,0:T(8,128)(2,1)S(1)}, u32[]{:S(2)}) copy-start(bf16[128,640]{1,0:T(8,128)(2,1)S(1)} %maximum_maximum_fusion.refs_9_) | copy-start | bytes 491524
  2.8 16.4 %collective-permute-start.3 = (bf16[128,640]{1,0:T(8,128)(2,1)S(1)}, bf16[128,640]{1,0:T(8,128)(2,1)S(1)}, u32[]{:S(2)}, u32[]{:S(2)}) collective-permute-start(bf16[128,640]{1,0:T(8,128)(2,1)S(1)} %maximum_maximum_fusion.refs_9_), channel_id=1, source_target_pairs={{0,8},{8,16},{16,24},{24,32},{32,40},{40,48},{48,56},{56,64},{64,7... | collective-permute-start | bytes 491528 | tf_op jit(solution)/shard_map/ppermute | solution.py:215
  4.6 14.6 %collective-permute-start.2 = (bf16[128,640]{1,0:T(8,128)(2,1)S(1)}, bf16[128,640]{1,0:T(8,128)(2,1)S(1)}, u32[]{:S(2)}, u32[]{:S(2)}) collective-permute-start(bf16[128,640]{1,0:T(8,128)(2,1)S(1)} %maximum_maximum_fusion.refs_9_), channel_id=1, source_target_pairs={{0,16},{8,24},{16,32},{24,40},{32,48},{40,56},{48,64},{56,72},{64,... | collective-permute-start | bytes 491528 | tf_op jit(solution)/shard_map/ppermute | solution.py:215
  8.2 11.0 %collective-permute-start.1 = (bf16[128,640]{1,0:T(8,128)(2,1)S(1)}, bf16[128,640]{1,0:T(8,128)(2,1)S(1)}, u32[]{:S(2)}, u32[]{:S(2)}) collective-permute-start(bf16[128,640]{1,0:T(8,128)(2,1)S(1)} %maximum_maximum_fusion.refs_9_), channel_id=1, source_target_pairs={{0,24},{8,32},{16,40},{24,48},{32,56},{40,64},{48,72},{56,80},{64,... | collective-permute-start | bytes 491528 | tf_op jit(solution)/shard_map/ppermute | solution.py:215
  12.2 7.0 %collective-permute-start = (bf16[64,640]{1,0:T(8,128)(2,1)S(1)}, bf16[64,640]{1,0:T(8,128)(2,1)S(1)}, u32[]{:S(2)}, u32[]{:S(2)}) collective-permute-start(bf16[64,640]{1,0:T(8,128)(2,1)S(1)} %slice.75), channel_id=1, source_target_pairs={{0,32},{8,40},{16,48},{24,56},{32,64},{40,72},{48,80},{56,88},{64,... | collective-permute-start | bytes 245768 | tf_op jit(solution)/shard_map/ppermute | solution.py:215
  19.2 0.6 copy-start.4
  19.2 0.7 copy-start.1
  19.2 0.7 copy-start.2
  20.0 0.7 copy-start.3
  38.5 24.3 %collective-permute-start.12 = (bf16[2,256,2048]{2,1,0:T(8,128)(2,1)}, bf16[2,256,2048]{2,1,0:T(8,128)(2,1)S(1)}, u32[]{:S(2)}, u32[]{:S(2)}) collective-permute-start(bf16[2,256,2048]{2,1,0:T(8,128)(2,1)} %get-tuple-element.22), channel_id=1, source_target_pairs={{0,8},{8,0},{16,24},{24,16},{32,40},{40,32},{48,56},{56,48},{64,72... | collective-permute-start | bytes 6291464 | tf_op jit(solution)/shard_map/ppermute | solution.py:219
  38.6 15.2 %collective-permute-start.4 = (bf16[128,576]{1,0:T(8,128)(2,1)}, bf16[128,576]{1,0:T(8,128)(2,1)S(1)}, u32[]{:S(2)}, u32[]{:S(2)}) collective-permute-start(bf16[128,576]{1,0:T(8,128)(2,1)} %get-tuple-element.17), channel_id=1, source_target_pairs={{8,0},{16,8},{24,16},{32,24},{40,32},{48,40},{56,48},{64,56},{72,6... | collective-permute-start | bytes 442376 | tf_op jit(solution)/shard_map/ppermute | solution.py:215
  39.9 13.9 %collective-permute-start.5 = (bf16[128,576]{1,0:T(8,128)(2,1)}, bf16[128,576]{1,0:T(8,128)(2,1)S(1)}, u32[]{:S(2)}, u32[]{:S(2)}) collective-permute-start(bf16[128,576]{1,0:T(8,128)(2,1)} %get-tuple-element.18), channel_id=1, source_target_pairs={{16,0},{24,8},{32,16},{40,24},{48,32},{56,40},{64,48},{72,56},{80,... | collective-permute-start | bytes 442376 | tf_op jit(solution)/shard_map/ppermute | solution.py:215
  41.2 12.6 %collective-permute-start.6 = (bf16[128,576]{1,0:T(8,128)(2,1)}, bf16[128,576]{1,0:T(8,128)(2,1)S(1)}, u32[]{:S(2)}, u32[]{:S(2)}) collective-permute-start(bf16[128,576]{1,0:T(8,128)(2,1)} %get-tuple-element.19), channel_id=1, source_target_pairs={{24,0},{32,8},{40,16},{48,24},{56,32},{64,40},{72,48},{80,56},{88,... | collective-permute-start | bytes 442376 | tf_op jit(solution)/shard_map/ppermute | solution.py:215
  42.5 11.3 %collective-permute-start.7 = (bf16[64,576]{1,0:T(8,128)(2,1)}, bf16[64,576]{1,0:T(8,128)(2,1)S(1)}, u32[]{:S(2)}, u32[]{:S(2)}) collective-permute-start(bf16[64,576]{1,0:T(8,128)(2,1)} %get-tuple-element.20), channel_id=1, source_target_pairs={{32,0},{40,8},{48,16},{56,24},{64,32},{72,40},{80,48},{88,56},{96,... | collective-permute-start | bytes 221192 | tf_op jit(solution)/shard_map/ppermute | solution.py:215
  54.8 4.5 %collective-permute-start.8 = (bf16[64,576]{1,0:T(8,128)(2,1)S(1)}, bf16[64,576]{1,0:T(8,128)(2,1)S(1)}, u32[]{:S(2)}, u32[]{:S(2)}) collective-permute-start(bf16[64,576]{1,0:T(8,128)(2,1)S(1)} %select_convert_fusion), channel_id=1, source_target_pairs={{0,1},{1,0},{2,3},{3,2},{4,5},{5,4},{6,7},{7,6},{8,9},{9,8},{10,11... | collective-permute-start | bytes 221192 | tf_op jit(solution)/shard_map/ppermute | solution.py:236
  59.4 14.0 %collective-permute-start.9 = (bf16[64,576]{1,0:T(8,128)(2,1)S(1)}, bf16[64,576]{1,0:T(8,128)(2,1)S(1)}, u32[]{:S(2)}, u32[]{:S(2)}) collective-permute-start(bf16[64,576]{1,0:T(8,128)(2,1)S(1)} %add_convert_fusion.4), channel_id=1, source_target_pairs={{0,2},{1,3},{2,0},{3,1},{4,6},{5,7},{6,4},{7,5},{8,10},{9,11},{10,... | collective-permute-start | bytes 221192 | tf_op jit(solution)/shard_map/ppermute | solution.py:236
  65.2 15.7 %collective-permute-start.13 = (bf16[2,64,2048]{2,1,0:T(8,128)(2,1)S(1)}, bf16[2,64,2048]{2,1,0:T(8,128)(2,1)S(1)}, u32[]{:S(2)}, u32[]{:S(2)}) collective-permute-start(bf16[2,64,2048]{2,1,0:T(8,128)(2,1)S(1)} %get-tuple-element.30), channel_id=1, source_target_pairs={{0,32},{8,136},{16,48},{24,152},{32,0},{40,168},{48,16},{56,184},{... | collective-permute-start | bytes 1572872 | tf_op jit(solution)/shard_map/ppermute | solution.py:226
  70.1 14.8 %collective-permute-start.15 = (bf16[2,64,2048]{2,1,0:T(8,128)(2,1)S(1)}, bf16[2,64,2048]{2,1,0:T(8,128)(2,1)S(1)}, u32[]{:S(2)}, u32[]{:S(2)}) collective-permute-start(bf16[2,64,2048]{2,1,0:T(8,128)(2,1)S(1)} %get-tuple-element.31), channel_id=1, source_target_pairs={{0,48},{8,200},{16,32},{24,216},{32,16},{40,232},{48,0},{56,248},{... | collective-permute-start | bytes 1572872 | tf_op jit(solution)/shard_map/ppermute | solution.py:226
  72.6 13.6 %collective-permute-start.14 = (bf16[2,64,2048]{2,1,0:T(8,128)(2,1)S(1)}, bf16[2,64,2048]{2,1,0:T(8,128)(2,1)S(1)}, u32[]{:S(2)}, u32[]{:S(2)}) collective-permute-start(bf16[2,64,2048]{2,1,0:T(8,128)(2,1)S(1)} %get-tuple-element.32), channel_id=1, source_target_pairs={{0,16},{8,72},{16,0},{24,88},{32,48},{40,104},{48,32},{56,120},{64... | collective-permute-start | bytes 1572872 | tf_op jit(solution)/shard_map/ppermute | solution.py:226
  73.4 7.4 %collective-permute-start.10 = (bf16[64,576]{1,0:T(8,128)(2,1)S(1)}, bf16[64,576]{1,0:T(8,128)(2,1)S(1)}, u32[]{:S(2)}, u32[]{:S(2)}) collective-permute-start(bf16[64,576]{1,0:T(8,128)(2,1)S(1)} %add_convert_fusion.3), channel_id=1, source_target_pairs={{0,6},{1,7},{2,4},{3,5},{4,2},{5,3},{6,0},{7,1},{8,14},{9,15},{10,... | collective-permute-start | bytes 221192 | tf_op jit(solution)/shard_map/ppermute | solution.py:236
  80.8 10.1 %collective-permute-start.11 = (bf16[64,576]{1,0:T(8,128)(2,1)S(1)}, bf16[64,576]{1,0:T(8,128)(2,1)S(1)}, u32[]{:S(2)}, u32[]{:S(2)}) collective-permute-start(bf16[64,576]{1,0:T(8,128)(2,1)S(1)} %add_convert_fusion.2), channel_id=1, source_target_pairs={{0,1},{1,0},{2,3},{3,2},{4,5},{5,4},{6,7},{7,6},{8,9},{9,8},{10,11... | collective-permute-start | bytes 221192 | tf_op jit(solution)/shard_map/ppermute | solution.py:236
  86.6 6.6 %collective-permute-start.16 = (bf16[2,16,2048]{2,1,0:T(8,128)(2,1)S(1)}, bf16[2,16,2048]{2,1,0:T(8,128)(2,1)S(1)}, u32[]{:S(2)}, u32[]{:S(2)}) collective-permute-start(bf16[2,16,2048]{2,1,0:T(8,128)(2,1)S(1)} %get-tuple-element.35), channel_id=1, source_target_pairs={{0,128},{8,40},{16,144},{24,56},{32,160},{40,8},{48,176},{56,24},{... | collective-permute-start | bytes 393224 | tf_op jit(solution)/shard_map/ppermute | solution.py:226
  89.8 6.2 %collective-permute-start.18 = (bf16[2,16,2048]{2,1,0:T(8,128)(2,1)S(1)}, bf16[2,16,2048]{2,1,0:T(8,128)(2,1)S(1)}, u32[]{:S(2)}, u32[]{:S(2)}) collective-permute-start(bf16[2,16,2048]{2,1,0:T(8,128)(2,1)S(1)} %get-tuple-element.36), channel_id=1, source_target_pairs={{0,192},{8,56},{16,208},{24,40},{32,224},{40,24},{48,240},{56,8},{... | collective-permute-start | bytes 393224 | tf_op jit(solution)/shard_map/ppermute | solution.py:226
  90.9 5.1 %collective-permute-start.17 = (bf16[2,16,2048]{2,1,0:T(8,128)(2,1)S(1)}, bf16[2,16,2048]{2,1,0:T(8,128)(2,1)S(1)}, u32[]{:S(2)}, u32[]{:S(2)}) collective-permute-start(bf16[2,16,2048]{2,1,0:T(8,128)(2,1)S(1)} %get-tuple-element.37), channel_id=1, source_target_pairs={{0,64},{8,24},{16,80},{24,8},{32,96},{40,56},{48,112},{56,40},{64,... | collective-permute-start | bytes 393224 | tf_op jit(solution)/shard_map/ppermute | solution.py:226

commit v4 on v3

--- a/solution.py
+++ b/solution.py
@@ -203,7 +203,7 @@
             pltpu.VMEM((heads, TOK, ROPE), f32),
             pltpu.VMEM((WINDOW, WIDE), f32),
         ],
-        compiler_params=pltpu.CompilerParams(vmem_limit_bytes=54 * 2**20),
+        compiler_params=pltpu.CompilerParams(vmem_limit_bytes=40 * 2**20),
         cost_estimate=pl.CostEstimate(
             flops=int(18e9), bytes_accessed=16 * 2**20, transcendentals=2 * steps * rows * SEEN
         ),

time: 97.4 us -> 98.7 us (1.013)
  local copies, waits for them, and re-layouts: 4.44 us -> 7.86 us
  Pallas kernels: 17.8 us -> 16 us
    unnamed x12 -> x10, local copies, waits for them, and re-layouts: 3.31 us -> 7.28 us
    pallas_call x1, Pallas kernels: 17.8 us -> 16 us  [attend(): pl.pallas_call(functools.partial(attend_kernel, heads), grid=(steps,), in...]
  transfers between devices with their start and end apart: 19 -> 19, of which waited for: 8 -> 8; matrix products, arithmetic and copies ran while one was open for 6% -> 4% of each run, Pallas kernels for 0% -> 0%
where the time goes in v4:
time: 98.7 us; the launch traced here: 98 us
  starting transfers between devices  39.5 us (40%)
  waiting for transfers between devices  29.2 us (30%)
  Pallas kernels  16 us (16%)
  local copies, waits for them, and re-layouts  7.86 us (8%)
  other arithmetic  4.47 us (5%)
    ppermute x8, starting transfers between devices, passed_along(): return lax.ppermute(x, 'ctx', pairs)  19.4 us
    pallas_call x1, Pallas kernels, attend(): pl.pallas_call(functools.partial(attend_kernel, heads), grid=(steps,), in...  16 us
    ppermute x6, starting transfers between devices, over_ring(): lax.ppermute(x[:, n * q:(n + 1) * q], 'ctx', ring_pairs(turn, step))  12.7 us
    ppermute x8, waiting for transfers between devices, passed_along(): return lax.ppermute(x, 'ctx', pairs)  11.7 us
    ppermute x6, waiting for transfers between devices, over_ring(): lax.ppermute(x[:, n * q:(n + 1) * q], 'ctx', ring_pairs(turn, step))  9.41 us
    ppermute x4, waiting for transfers between devices, sum_over_head(): swap = lambda y, d: lax.ppermute(y, 'head', [(i, i ^ d) for i in range(8)])  8.1 us
    ppermute x4, starting transfers between devices, sum_over_head(): swap = lambda y, d: lax.ppermute(y, 'head', [(i, i ^ d) for i in range(8)])  7.34 us
    unnamed x10, local copies, waits for them, and re-layouts  7.28 us
  transfers between devices with their start and end apart: 19, of which 8 were waited for; matrix products, arithmetic and copies ran while one was open for 4% of the time, Pallas kernels for 0%

profile of v4, /device:TPU:32, one launch (start us, length us, event | category | flops | bytes accessed | tf_op | source)
XLA Modules:
  0.0 98.0 jit_solution(11780605327157906135)
XLA Ops:
  0.6 0.7 convert_bitcast_fusion
  1.3 0.1 copy.13
  1.4 0.1 copy.12
  1.6 1.1 %copy.11 = bf16[128,576]{1,0:T(8,128)(2,1)S(1)} copy(bf16[128,576]{0,1:T(8,128)(2,1)} %param.7) | data formatting | bytes 294912 | tf_op args[1]
  2.7 0.1 pad.7.clone
  2.7 0.1 maximum_maximum_fusion.refs_9_
  2.8 1.7 %collective-permute-start.3 = (bf16[128,640]{1,0:T(8,128)(2,1)S(1)}, bf16[128,640]{1,0:T(8,128)(2,1)S(1)}, u32[]{:S(2)}, u32[]{:S(2)}) collective-permute-start(bf16[128,640]{1,0:T(8,128)(2,1)S(1)} %maximum_maximum_fusion.refs_9_), channel_id=1, source_target_pairs={{0,8},{8,16},{16,24},{24,32},{32,40},{40,48},{48,56},{56,64},{64,7... | collective-permute-start | bytes 491528 | tf_op jit(solution)/shard_map/ppermute | solution.py:215
  4.6 3.6 %collective-permute-start.2 = (bf16[128,640]{1,0:T(8,128)(2,1)S(1)}, bf16[128,640]{1,0:T(8,128)(2,1)S(1)}, u32[]{:S(2)}, u32[]{:S(2)}) collective-permute-start(bf16[128,640]{1,0:T(8,128)(2,1)S(1)} %maximum_maximum_fusion.refs_9_), channel_id=1, source_target_pairs={{0,16},{8,24},{16,32},{24,40},{32,48},{40,56},{48,64},{56,72},{64,... | collective-permute-start | bytes 491528 | tf_op jit(solution)/shard_map/ppermute | solution.py:215
  8.2 4.0 %collective-permute-start.1 = (bf16[128,640]{1,0:T(8,128)(2,1)S(1)}, bf16[128,640]{1,0:T(8,128)(2,1)S(1)}, u32[]{:S(2)}, u32[]{:S(2)}) collective-permute-start(bf16[128,640]{1,0:T(8,128)(2,1)S(1)} %maximum_maximum_fusion.refs_9_), channel_id=1, source_target_pairs={{0,24},{8,32},{16,40},{24,48},{32,56},{40,64},{48,72},{56,80},{64,... | collective-permute-start | bytes 491528 | tf_op jit(solution)/shard_map/ppermute | solution.py:215
  12.2 4.9 %collective-permute-start = (bf16[64,640]{1,0:T(8,128)(2,1)S(1)}, bf16[64,640]{1,0:T(8,128)(2,1)S(1)}, u32[]{:S(2)}, u32[]{:S(2)}) collective-permute-start(bf16[64,640]{1,0:T(8,128)(2,1)S(1)} %slice.75), channel_id=1, source_target_pairs={{0,32},{8,40},{16,48},{24,56},{32,64},{40,72},{48,80},{56,88},{64,... | collective-permute-start | bytes 245768 | tf_op jit(solution)/shard_map/ppermute | solution.py:215
  17.2 0.1 concatenate.14.refs_0_
  17.3 1.9 %collective-permute-done.refs_5_ = bf16[64,640]{1,0:T(8,128)(2,1)S(1)} collective-permute-done((bf16[64,640]{1,0:T(8,128)(2,1)S(1)}, bf16[64,640]{1,0:T(8,128)(2,1)S(1)}, u32[]{:S(2)}, u32[]{:S(2)}) %collective-permute-start) | collective-permute-done | bytes 81952 | tf_op jit(solution)/shard_map/ppermute | solution.py:215
  19.2 0.0 collective-permute-done.3.refs_8_
  19.2 0.0 collective-permute-done.2.refs_7_
  19.2 0.0 collective-permute-done.1.refs_6_
  19.2 0.0 copy-start
  19.2 1.6 %copy-done = bf16[512,2048]{1,0:T(8,128)(2,1)S(1)} copy-done((bf16[512,2048]{1,0:T(8,128)(2,1)S(1)}, bf16[512,2048]{1,0:T(8,128)(2,1)}, u32[]{:S(2)}) %copy-start) | copy-done | bytes 2097176
  20.8 0.0 copy-start.1
  20.8 1.6 %copy-done.1 = bf16[512,2048]{1,0:T(8,128)(2,1)S(1)} copy-done((bf16[512,2048]{1,0:T(8,128)(2,1)S(1)}, bf16[512,2048]{1,0:T(8,128)(2,1)}, u32[]{:S(2)}) %copy-start.1) | copy-done | bytes 2097176
  22.4 0.0 copy-start.2
  22.4 1.1 %copy-done.2 = bf16[128,3072]{1,0:T(8,128)(2,1)S(1)} copy-done((bf16[128,3072]{1,0:T(8,128)(2,1)S(1)}, bf16[128,3072]{1,0:T(8,128)(2,1)}, u32[]{:S(2)}) %copy-start.2) | copy-done | bytes 786456
  23.5 0.0 copy-start.3
  23.5 1.0 %copy-done.3 = bf16[128,2048]{1,0:T(8,128)(2,1)S(1)} copy-done((bf16[128,2048]{1,0:T(8,128)(2,1)S(1)}, bf16[128,2048]{1,0:T(8,128)(2,1)}, u32[]{:S(2)}) %copy-start.3) | copy-done | bytes 524312
  24.6 16.0 %shard_map.101 = (bf16[128,2048]{1,0:T(8,128)(2,1)}, f32[128,3072]{1,0:T(8,128)}, bf16[2,256,2048]{2,1,0:T(8,128)(2,1)}, bf16[2,256,2048]{2,1,0:T(8,128)(2,1)S(1...) custom-call(s32[65]{0:T(128)S(1)} %concatenate.14.refs_0_, ...), custom_call_target="tpu_custom_call" | custom-call | flops 17999998976 | bytes 16777216 | tf_op jit(solution)/shard_map/pallas_call | solution.py:181
  40.6 0.1 collective-permute-start.12
  40.7 1.3 %collective-permute-start.4 = (bf16[128,576]{1,0:T(8,128)(2,1)}, bf16[128,576]{1,0:T(8,128)(2,1)S(1)}, u32[]{:S(2)}, u32[]{:S(2)}) collective-permute-start(bf16[128,576]{1,0:T(8,128)(2,1)} %get-tuple-element.17), channel_id=1, source_target_pairs={{8,0},{16,8},{24,16},{32,24},{40,32},{48,40},{56,48},{64,56},{72,6... | collective-permute-start | bytes 442376 | tf_op jit(solution)/shard_map/ppermute | solution.py:215
  42.0 1.3 %collective-permute-start.5 = (bf16[128,576]{1,0:T(8,128)(2,1)S(1)}, bf16[128,576]{1,0:T(8,128)(2,1)S(1)}, u32[]{:S(2)}, u32[]{:S(2)}) collective-permute-start(bf16[128,576]{1,0:T(8,128)(2,1)S(1)} %get-tuple-element.18), channel_id=1, source_target_pairs={{16,0},{24,8},{32,16},{40,24},{48,32},{56,40},{64,48},{72,56},{80,... | collective-permute-start | bytes 442376 | tf_op jit(solution)/shard_map/ppermute | solution.py:215
  43.3 1.3 %collective-permute-start.6 = (bf16[128,576]{1,0:T(8,128)(2,1)S(1)}, bf16[128,576]{1,0:T(8,128)(2,1)S(1)}, u32[]{:S(2)}, u32[]{:S(2)}) collective-permute-start(bf16[128,576]{1,0:T(8,128)(2,1)S(1)} %get-tuple-element.19), channel_id=1, source_target_pairs={{24,0},{32,8},{40,16},{48,24},{56,32},{64,40},{72,48},{80,56},{88,... | collective-permute-start | bytes 442376 | tf_op jit(solution)/shard_map/ppermute | solution.py:215
  44.6 1.3 %collective-permute-start.7 = (bf16[64,576]{1,0:T(8,128)(2,1)}, bf16[64,576]{1,0:T(8,128)(2,1)S(1)}, u32[]{:S(2)}, u32[]{:S(2)}) collective-permute-start(bf16[64,576]{1,0:T(8,128)(2,1)} %get-tuple-element.20), channel_id=1, source_target_pairs={{32,0},{40,8},{48,16},{56,24},{64,32},{72,40},{80,48},{88,56},{96,... | collective-permute-start | bytes 221192 | tf_op jit(solution)/shard_map/ppermute | solution.py:215
  45.9 9.8 %collective-permute-done.7 = bf16[64,576]{1,0:T(8,128)(2,1)S(1)} collective-permute-done((bf16[64,576]{1,0:T(8,128)(2,1)}, bf16[64,576]{1,0:T(8,128)(2,1)S(1)}, u32[]{:S(2)}, u32[]{:S(2)}) %collective-permute-start.7) | collective-permute-done | bytes 73760 | tf_op jit(solution)/shard_map/ppermute | solution.py:215
  55.7 0.0 collective-permute-done.4
  55.7 0.0 collective-permute-done.5
  55.7 0.0 collective-permute-done.6
  55.7 0.1 convert_add_fusion
  55.8 0.2 collective-permute-start.8
  56.0 4.3 %collective-permute-done.8 = bf16[64,576]{1,0:T(8,128)(2,1)S(1)} collective-permute-done((bf16[64,576]{1,0:T(8,128)(2,1)S(1)}, bf16[64,576]{1,0:T(8,128)(2,1)S(1)}, u32[]{:S(2)}, u32[]{:S(2)}) %collective-permute-start.8) | collective-permute-done | bytes 73760 | tf_op jit(solution)/shard_map/ppermute | solution.py:236
  60.4 3.4 %collective-permute-start.9 = (bf16[64,576]{1,0:T(8,128)(2,1)S(1)}, bf16[64,576]{1,0:T(8,128)(2,1)S(1)}, u32[]{:S(2)}, u32[]{:S(2)}) collective-permute-start(bf16[64,576]{1,0:T(8,128)(2,1)S(1)} %add_convert_fusion.4), channel_id=1, source_target_pairs={{0,2},{1,3},{2,0},{3,1},{4,6},{5,7},{6,4},{7,5},{8,10},{9,11},{10,... | collective-permute-start | bytes 221192 | tf_op jit(solution)/shard_map/ppermute | solution.py:236
  63.7 0.0 collective-permute-done.12
  63.7 2.4 %add_convert_fusion = bf16[2,256,2048]{2,1,0:T(8,128)(2,1)S(1)} fusion(bf16[2,256,2048]{2,1,0:T(8,128)(2,1)} %collective-permute-done.12, bf16[2,256,2048]{2,1,0:T(8,128)(2,1)S(1)} %get-tuple-element.21), kind=kLoop, calls=%fused_computation | loop fusion | flops 4194304 | bytes 6291456 | tf_op jit(solution)/shard_map/convert_element_type | solution.py:220
  66.1 0.1 fusion.6
  66.2 4.9 %collective-permute-start.13 = (bf16[2,64,2048]{2,1,0:T(8,128)(2,1)S(1)}, bf16[2,64,2048]{2,1,0:T(8,128)(2,1)S(1)}, u32[]{:S(2)}, u32[]{:S(2)}) collective-permute-start(bf16[2,64,2048]{2,1,0:T(8,128)(2,1)S(1)} %get-tuple-element.30), channel_id=1, source_target_pairs={{0,32},{8,136},{16,48},{24,152},{32,0},{40,168},{48,16},{56,184},{... | collective-permute-start | bytes 1572872 | tf_op jit(solution)/shard_map/ppermute | solution.py:226
  71.1 2.7 %collective-permute-start.15 = (bf16[2,64,2048]{2,1,0:T(8,128)(2,1)S(1)}, bf16[2,64,2048]{2,1,0:T(8,128)(2,1)S(1)}, u32[]{:S(2)}, u32[]{:S(2)}) collective-permute-start(bf16[2,64,2048]{2,1,0:T(8,128)(2,1)S(1)} %get-tuple-element.31), channel_id=1, source_target_pairs={{0,48},{8,200},{16,32},{24,216},{32,16},{40,232},{48,0},{56,248},{... | collective-permute-start | bytes 1572872 | tf_op jit(solution)/shard_map/ppermute | solution.py:226
  73.8 0.8 collective-permute-start.14
  74.6 0.0 collective-permute-done.9
  74.6 3.6 %collective-permute-start.10 = (bf16[64,576]{1,0:T(8,128)(2,1)S(1)}, bf16[64,576]{1,0:T(8,128)(2,1)S(1)}, u32[]{:S(2)}, u32[]{:S(2)}) collective-permute-start(bf16[64,576]{1,0:T(8,128)(2,1)S(1)} %add_convert_fusion.3), channel_id=1, source_target_pairs={{0,6},{1,7},{2,4},{3,5},{4,2},{5,3},{6,0},{7,1},{8,14},{9,15},{10,... | collective-permute-start | bytes 221192 | tf_op jit(solution)/shard_map/ppermute | solution.py:236
  78.2 3.8 %collective-permute-done.10 = bf16[64,576]{1,0:T(8,128)(2,1)S(1)} collective-permute-done((bf16[64,576]{1,0:T(8,128)(2,1)S(1)}, bf16[64,576]{1,0:T(8,128)(2,1)S(1)}, u32[]{:S(2)}, u32[]{:S(2)}) %collective-permute-start.10) | collective-permute-done | bytes 73760 | tf_op jit(solution)/shard_map/ppermute | solution.py:236
  82.0 0.1 collective-permute-start.11
  82.2 0.0 collective-permute-done.13
  82.2 4.0 %collective-permute-done.15 = bf16[2,64,2048]{2,1,0:T(8,128)(2,1)S(1)} collective-permute-done((bf16[2,64,2048]{2,1,0:T(8,128)(2,1)S(1)}, bf16[2,64,2048]{2,1,0:T(8,128)(2,1)S(1)}, u32[]{:S(2)}, u32[]{:S(2)}) %collective-permute-start.15) | collective-permute-done | bytes 524320 | tf_op jit(solution)/shard_map/ppermute | solution.py:226
  86.1 1.3 %collective-permute-done.14 = bf16[2,64,2048]{2,1,0:T(8,128)(2,1)S(1)} collective-permute-done((bf16[2,64,2048]{2,1,0:T(8,128)(2,1)S(1)}, bf16[2,64,2048]{2,1,0:T(8,128)(2,1)S(1)}, u32[]{:S(2)}, u32[]{:S(2)}) %collective-permute-start.14) | collective-permute-done | bytes 524320 | tf_op jit(solution)/shard_map/ppermute | solution.py:226
  87.4 0.3 add_convert_fusion.1
  87.8 3.3 %collective-permute-start.16 = (bf16[2,16,2048]{2,1,0:T(8,128)(2,1)S(1)}, bf16[2,16,2048]{2,1,0:T(8,128)(2,1)S(1)}, u32[]{:S(2)}, u32[]{:S(2)}) collective-permute-start(bf16[2,16,2048]{2,1,0:T(8,128)(2,1)S(1)} %get-tuple-element.35), channel_id=1, source_target_pairs={{0,128},{8,40},{16,144},{24,56},{32,160},{40,8},{48,176},{56,24},{... | collective-permute-start | bytes 393224 | tf_op jit(solution)/shard_map/ppermute | solution.py:226
  91.0 1.1 %collective-permute-start.18 = (bf16[2,16,2048]{2,1,0:T(8,128)(2,1)S(1)}, bf16[2,16,2048]{2,1,0:T(8,128)(2,1)S(1)}, u32[]{:S(2)}, u32[]{:S(2)}) collective-permute-start(bf16[2,16,2048]{2,1,0:T(8,128)(2,1)S(1)} %get-tuple-element.36), channel_id=1, source_target_pairs={{0,192},{8,56},{16,208},{24,40},{32,224},{40,24},{48,240},{56,8},{... | collective-permute-start | bytes 393224 | tf_op jit(solution)/shard_map/ppermute | solution.py:226
  92.1 0.0 collective-permute-start.17
  92.1 0.0 collective-permute-done.11
  92.1 0.9 copy.14
  93.0 1.3 %collective-permute-done.16 = bf16[2,16,2048]{2,1,0:T(8,128)(2,1)S(1)} collective-permute-done((bf16[2,16,2048]{2,1,0:T(8,128)(2,1)S(1)}, bf16[2,16,2048]{2,1,0:T(8,128)(2,1)S(1)}, u32[]{:S(2)}, u32[]{:S(2)}) %collective-permute-start.16) | collective-permute-done | bytes 131104 | tf_op jit(solution)/shard_map/ppermute | solution.py:226
  94.3 2.9 %collective-permute-done.18 = bf16[2,16,2048]{2,1,0:T(8,128)(2,1)S(1)} collective-permute-done((bf16[2,16,2048]{2,1,0:T(8,128)(2,1)S(1)}, bf16[2,16,2048]{2,1,0:T(8,128)(2,1)S(1)}, u32[]{:S(2)}, u32[]{:S(2)}) %collective-permute-start.18) | collective-permute-done | bytes 131104 | tf_op jit(solution)/shard_map/ppermute | solution.py:226
  97.2 0.0 collective-permute-done.17
  97.2 0.8 add_bitcast_fusion
  (11 shorter events, 0.2 us)
Async XLA Ops:
  2.8 16.4 %collective-permute-start.3 = (bf16[128,640]{1,0:T(8,128)(2,1)S(1)}, bf16[128,640]{1,0:T(8,128)(2,1)S(1)}, u32[]{:S(2)}, u32[]{:S(2)}) collective-permute-start(bf16[128,640]{1,0:T(8,128)(2,1)S(1)} %maximum_maximum_fusion.refs_9_), channel_id=1, source_target_pairs={{0,8},{8,16},{16,24},{24,32},{32,40},{40,48},{48,56},{56,64},{64,7... | collective-permute-start | bytes 491528 | tf_op jit(solution)/shard_map/ppermute | solution.py:215
  4.6 14.6 %collective-permute-start.2 = (bf16[128,640]{1,0:T(8,128)(2,1)S(1)}, bf16[128,640]{1,0:T(8,128)(2,1)S(1)}, u32[]{:S(2)}, u32[]{:S(2)}) collective-permute-start(bf16[128,640]{1,0:T(8,128)(2,1)S(1)} %maximum_maximum_fusion.refs_9_), channel_id=1, source_target_pairs={{0,16},{8,24},{16,32},{24,40},{32,48},{40,56},{48,64},{56,72},{64,... | collective-permute-start | bytes 491528 | tf_op jit(solution)/shard_map/ppermute | solution.py:215
  8.2 11.0 %collective-permute-start.1 = (bf16[128,640]{1,0:T(8,128)(2,1)S(1)}, bf16[128,640]{1,0:T(8,128)(2,1)S(1)}, u32[]{:S(2)}, u32[]{:S(2)}) collective-permute-start(bf16[128,640]{1,0:T(8,128)(2,1)S(1)} %maximum_maximum_fusion.refs_9_), channel_id=1, source_target_pairs={{0,24},{8,32},{16,40},{24,48},{32,56},{40,64},{48,72},{56,80},{64,... | collective-permute-start | bytes 491528 | tf_op jit(solution)/shard_map/ppermute | solution.py:215
  12.2 7.0 %collective-permute-start = (bf16[64,640]{1,0:T(8,128)(2,1)S(1)}, bf16[64,640]{1,0:T(8,128)(2,1)S(1)}, u32[]{:S(2)}, u32[]{:S(2)}) collective-permute-start(bf16[64,640]{1,0:T(8,128)(2,1)S(1)} %slice.75), channel_id=1, source_target_pairs={{0,32},{8,40},{16,48},{24,56},{32,64},{40,72},{48,80},{56,88},{64,... | collective-permute-start | bytes 245768 | tf_op jit(solution)/shard_map/ppermute | solution.py:215
  19.2 1.6 %copy-start = (bf16[512,2048]{1,0:T(8,128)(2,1)S(1)}, bf16[512,2048]{1,0:T(8,128)(2,1)}, u32[]{:S(2)}) copy-start(bf16[512,2048]{1,0:T(8,128)(2,1)} %refs_3_.1) | copy-start | bytes 6291460
  20.8 1.6 %copy-start.1 = (bf16[512,2048]{1,0:T(8,128)(2,1)S(1)}, bf16[512,2048]{1,0:T(8,128)(2,1)}, u32[]{:S(2)}) copy-start(bf16[512,2048]{1,0:T(8,128)(2,1)} %refs_4_.1) | copy-start | bytes 6291460
  22.4 1.1 %copy-start.2 = (bf16[128,3072]{1,0:T(8,128)(2,1)S(1)}, bf16[128,3072]{1,0:T(8,128)(2,1)}, u32[]{:S(2)}) copy-start(bf16[128,3072]{1,0:T(8,128)(2,1)} %refs_1_.1) | copy-start | bytes 2359300
  23.5 1.0 %copy-start.3 = (bf16[128,2048]{1,0:T(8,128)(2,1)S(1)}, bf16[128,2048]{1,0:T(8,128)(2,1)}, u32[]{:S(2)}) copy-start(bf16[128,2048]{1,0:T(8,128)(2,1)} %refs_2_.1) | copy-start | bytes 1572868
  40.6 23.1 %collective-permute-start.12 = (bf16[2,256,2048]{2,1,0:T(8,128)(2,1)}, bf16[2,256,2048]{2,1,0:T(8,128)(2,1)}, u32[]{:S(2)}, u32[]{:S(2)}) collective-permute-start(bf16[2,256,2048]{2,1,0:T(8,128)(2,1)} %get-tuple-element.22), channel_id=1, source_target_pairs={{0,8},{8,0},{16,24},{24,16},{32,40},{40,32},{48,56},{56,48},{64,72... | collective-permute-start | bytes 6291464 | tf_op jit(solution)/shard_map/ppermute | solution.py:219
  40.7 15.0 %collective-permute-start.4 = (bf16[128,576]{1,0:T(8,128)(2,1)}, bf16[128,576]{1,0:T(8,128)(2,1)S(1)}, u32[]{:S(2)}, u32[]{:S(2)}) collective-permute-start(bf16[128,576]{1,0:T(8,128)(2,1)} %get-tuple-element.17), channel_id=1, source_target_pairs={{8,0},{16,8},{24,16},{32,24},{40,32},{48,40},{56,48},{64,56},{72,6... | collective-permute-start | bytes 442376 | tf_op jit(solution)/shard_map/ppermute | solution.py:215
  42.0 13.7 %collective-permute-start.5 = (bf16[128,576]{1,0:T(8,128)(2,1)S(1)}, bf16[128,576]{1,0:T(8,128)(2,1)S(1)}, u32[]{:S(2)}, u32[]{:S(2)}) collective-permute-start(bf16[128,576]{1,0:T(8,128)(2,1)S(1)} %get-tuple-element.18), channel_id=1, source_target_pairs={{16,0},{24,8},{32,16},{40,24},{48,32},{56,40},{64,48},{72,56},{80,... | collective-permute-start | bytes 442376 | tf_op jit(solution)/shard_map/ppermute | solution.py:215
  43.3 12.4 %collective-permute-start.6 = (bf16[128,576]{1,0:T(8,128)(2,1)S(1)}, bf16[128,576]{1,0:T(8,128)(2,1)S(1)}, u32[]{:S(2)}, u32[]{:S(2)}) collective-permute-start(bf16[128,576]{1,0:T(8,128)(2,1)S(1)} %get-tuple-element.19), channel_id=1, source_target_pairs={{24,0},{32,8},{40,16},{48,24},{56,32},{64,40},{72,48},{80,56},{88,... | collective-permute-start | bytes 442376 | tf_op jit(solution)/shard_map/ppermute | solution.py:215
  44.6 11.1 %collective-permute-start.7 = (bf16[64,576]{1,0:T(8,128)(2,1)}, bf16[64,576]{1,0:T(8,128)(2,1)S(1)}, u32[]{:S(2)}, u32[]{:S(2)}) collective-permute-start(bf16[64,576]{1,0:T(8,128)(2,1)} %get-tuple-element.20), channel_id=1, source_target_pairs={{32,0},{40,8},{48,16},{56,24},{64,32},{72,40},{80,48},{88,56},{96,... | collective-permute-start | bytes 221192 | tf_op jit(solution)/shard_map/ppermute | solution.py:215
  55.8 4.5 %collective-permute-start.8 = (bf16[64,576]{1,0:T(8,128)(2,1)S(1)}, bf16[64,576]{1,0:T(8,128)(2,1)S(1)}, u32[]{:S(2)}, u32[]{:S(2)}) collective-permute-start(bf16[64,576]{1,0:T(8,128)(2,1)S(1)} %select_convert_fusion), channel_id=1, source_target_pairs={{0,1},{1,0},{2,3},{3,2},{4,5},{5,4},{6,7},{7,6},{8,9},{9,8},{10,11... | collective-permute-start | bytes 221192 | tf_op jit(solution)/shard_map/ppermute | solution.py:236
  60.4 14.2 %collective-permute-start.9 = (bf16[64,576]{1,0:T(8,128)(2,1)S(1)}, bf16[64,576]{1,0:T(8,128)(2,1)S(1)}, u32[]{:S(2)}, u32[]{:S(2)}) collective-permute-start(bf16[64,576]{1,0:T(8,128)(2,1)S(1)} %add_convert_fusion.4), channel_id=1, source_target_pairs={{0,2},{1,3},{2,0},{3,1},{4,6},{5,7},{6,4},{7,5},{8,10},{9,11},{10,... | collective-permute-start | bytes 221192 | tf_op jit(solution)/shard_map/ppermute | solution.py:236
  66.2 15.9 %collective-permute-start.13 = (bf16[2,64,2048]{2,1,0:T(8,128)(2,1)S(1)}, bf16[2,64,2048]{2,1,0:T(8,128)(2,1)S(1)}, u32[]{:S(2)}, u32[]{:S(2)}) collective-permute-start(bf16[2,64,2048]{2,1,0:T(8,128)(2,1)S(1)} %get-tuple-element.30), channel_id=1, source_target_pairs={{0,32},{8,136},{16,48},{24,152},{32,0},{40,168},{48,16},{56,184},{... | collective-permute-start | bytes 1572872 | tf_op jit(solution)/shard_map/ppermute | solution.py:226
  71.1 15.0 %collective-permute-start.15 = (bf16[2,64,2048]{2,1,0:T(8,128)(2,1)S(1)}, bf16[2,64,2048]{2,1,0:T(8,128)(2,1)S(1)}, u32[]{:S(2)}, u32[]{:S(2)}) collective-permute-start(bf16[2,64,2048]{2,1,0:T(8,128)(2,1)S(1)} %get-tuple-element.31), channel_id=1, source_target_pairs={{0,48},{8,200},{16,32},{24,216},{32,16},{40,232},{48,0},{56,248},{... | collective-permute-start | bytes 1572872 | tf_op jit(solution)/shard_map/ppermute | solution.py:226
  73.8 13.6 %collective-permute-start.14 = (bf16[2,64,2048]{2,1,0:T(8,128)(2,1)S(1)}, bf16[2,64,2048]{2,1,0:T(8,128)(2,1)S(1)}, u32[]{:S(2)}, u32[]{:S(2)}) collective-permute-start(bf16[2,64,2048]{2,1,0:T(8,128)(2,1)S(1)} %get-tuple-element.32), channel_id=1, source_target_pairs={{0,16},{8,72},{16,0},{24,88},{32,48},{40,104},{48,32},{56,120},{64... | collective-permute-start | bytes 1572872 | tf_op jit(solution)/shard_map/ppermute | solution.py:226
  74.6 7.4 %collective-permute-start.10 = (bf16[64,576]{1,0:T(8,128)(2,1)S(1)}, bf16[64,576]{1,0:T(8,128)(2,1)S(1)}, u32[]{:S(2)}, u32[]{:S(2)}) collective-permute-start(bf16[64,576]{1,0:T(8,128)(2,1)S(1)} %add_convert_fusion.3), channel_id=1, source_target_pairs={{0,6},{1,7},{2,4},{3,5},{4,2},{5,3},{6,0},{7,1},{8,14},{9,15},{10,... | collective-permute-start | bytes 221192 | tf_op jit(solution)/shard_map/ppermute | solution.py:236
  82.0 10.0 %collective-permute-start.11 = (bf16[64,576]{1,0:T(8,128)(2,1)S(1)}, bf16[64,576]{1,0:T(8,128)(2,1)S(1)}, u32[]{:S(2)}, u32[]{:S(2)}) collective-permute-start(bf16[64,576]{1,0:T(8,128)(2,1)S(1)} %add_convert_fusion.2), channel_id=1, source_target_pairs={{0,1},{1,0},{2,3},{3,2},{4,5},{5,4},{6,7},{7,6},{8,9},{9,8},{10,11... | collective-permute-start | bytes 221192 | tf_op jit(solution)/shard_map/ppermute | solution.py:236
  87.8 6.6 %collective-permute-start.16 = (bf16[2,16,2048]{2,1,0:T(8,128)(2,1)S(1)}, bf16[2,16,2048]{2,1,0:T(8,128)(2,1)S(1)}, u32[]{:S(2)}, u32[]{:S(2)}) collective-permute-start(bf16[2,16,2048]{2,1,0:T(8,128)(2,1)S(1)} %get-tuple-element.35), channel_id=1, source_target_pairs={{0,128},{8,40},{16,144},{24,56},{32,160},{40,8},{48,176},{56,24},{... | collective-permute-start | bytes 393224 | tf_op jit(solution)/shard_map/ppermute | solution.py:226
  91.0 6.2 %collective-permute-start.18 = (bf16[2,16,2048]{2,1,0:T(8,128)(2,1)S(1)}, bf16[2,16,2048]{2,1,0:T(8,128)(2,1)S(1)}, u32[]{:S(2)}, u32[]{:S(2)}) collective-permute-start(bf16[2,16,2048]{2,1,0:T(8,128)(2,1)S(1)} %get-tuple-element.36), channel_id=1, source_target_pairs={{0,192},{8,56},{16,208},{24,40},{32,224},{40,24},{48,240},{56,8},{... | collective-permute-start | bytes 393224 | tf_op jit(solution)/shard_map/ppermute | solution.py:226
  92.1 5.1 %collective-permute-start.17 = (bf16[2,16,2048]{2,1,0:T(8,128)(2,1)S(1)}, bf16[2,16,2048]{2,1,0:T(8,128)(2,1)S(1)}, u32[]{:S(2)}, u32[]{:S(2)}) collective-permute-start(bf16[2,16,2048]{2,1,0:T(8,128)(2,1)S(1)} %get-tuple-element.37), channel_id=1, source_target_pairs={{0,64},{8,24},{16,80},{24,8},{32,96},{40,56},{48,112},{56,40},{64,... | collective-permute-start | bytes 393224 | tf_op jit(solution)/shard_map/ppermute | solution.py:226
